TPU v7x, 128 devices: a whole 4x4x4 slice. The times are simulated.
128 devices in a mesh: index: 16 (over y, x), query: 8 (over z, core).
Axes of the slice: x: 4, y: 4, z: 4, core: 2. Of those that a mesh axis runs over, the one named last changes fastest.
Arguments:
- queries: bfloat16 [1024, 2048], P(('index', 'query')), may hold values from -4 to 4
- slab: bfloat16 [524288, 2048], P(('index', 'query')), may hold values from -24 to 24
- cand_owner: int32 [1024, 32], P(('index', 'query')), may hold values from 0 to 127, all different within a row; in each aligned block of 8 rows (0 to 7, 8 to 15, ...) at most 4 rows name the same one
- cand_row: int32 [1024, 32], P(('index', 'query')), may hold values from 0 to 4095
Outputs:
- pooled: float32 [1024, 256], P(('index', 'query'))
- coarse_lse: float32 [1024], P(('index', 'query'))
- margin: float32 [1024, 32], P(('index', 'query'))
Inputs may be any that keep to these rules, and one draw needn't show every extreme that they name: `cand_owner`: each query names 32 distinct owners. Over the 8 queries of one device (aligned blocks of 8 rows) no owner is named more than 4 times, a bound that some block reaches.
All inputs are finite; a program needn't handle non-finite values.
Results may differ from a plain program's by a relative error of at most 0.00165.
Values may be sent and summed in bfloat16 or wider, within the bound.
A program may use at most 128 MiB of HBM per device.

v0:
```python
import jax
import jax.numpy as jnp
from jax import lax
from jax.sharding import PartitionSpec as P

PREFIX = 256


def on_device(queries, slab, cand_owner, cand_row):
    q_dev = queries.shape[0]
    width = slab.shape[1]
    owners = lax.axis_size(("index", "query"))
    k_count = cand_owner.shape[1]
    prefix_keys = slab[:, :PREFIX]
    scale = PREFIX ** (-0.5)
    logits = (
        lax.dot_general(
            lax.all_gather(queries[:, :PREFIX], ("index", "query"), axis=0, tiled=True),
            prefix_keys,
            (((1,), (1,)), ((), ())),
            preferred_element_type=jnp.float32,
        )
        * scale
    )
    top = lax.pmax(jnp.max(logits, axis=1), ("index", "query"))
    weights = jnp.exp(logits - top[:, None])
    parts = (
        jnp.dot(weights.astype(jnp.bfloat16), prefix_keys, preferred_element_type=jnp.float32),
        jnp.sum(weights, axis=1),
    )
    results = lax.psum_scatter(parts, ("index", "query"), scatter_dimension=0, tiled=True)
    pooled_sum = results[0]
    total = results[1]
    my_start = lax.axis_index(("index", "query")) * q_dev
    my_top = lax.dynamic_slice_in_dim(top, my_start, q_dev, 0)
    pooled = pooled_sum / total[:, None]
    coarse_lse = my_top + jnp.log(total)
    capacity = max(2, min(q_dev, 2 * q_dev * k_count // owners))
    flat_owner = cand_owner.reshape(-1)
    flat_row = cand_row.reshape(-1)
    hits = (flat_owner[:, None] == jnp.arange(owners, dtype=jnp.int32)[None, :]).astype(jnp.int32)
    earlier = jnp.cumsum(hits, axis=0) - hits
    slot = jnp.sum(earlier * hits, axis=1)
    target = flat_owner * capacity + slot
    request = jnp.zeros((owners * capacity,), jnp.int32).at[target].set(flat_row)
    fetched = lax.all_to_all(
        slab[
            lax.all_to_all(
                request.reshape(owners, capacity),
                ("index", "query"),
                split_axis=0,
                concat_axis=0,
                tiled=True,
            )
        ],
        ("index", "query"),
        split_axis=0,
        concat_axis=0,
        tiled=True,
    )
    cand_rows = fetched.reshape(owners * capacity, width)[target].reshape(q_dev, k_count, width)
    full = jnp.einsum(
        "qw,qkw->qk", queries, cand_rows, preferred_element_type=jnp.float32
    ) * width ** (-0.5)
    margin = full - coarse_lse[:, None]
    return (pooled, coarse_lse, margin)


def solution(mesh):
    in_specs = (
        P(("index", "query"), None),
        P(("index", "query"), None),
        P(("index", "query"), None),
        P(("index", "query"), None),
    )
    out_specs = (P(("index", "query"), None), P(("index", "query")), P(("index", "query"), None))
    return jax.shard_map(
        on_device, mesh=mesh, in_specs=in_specs, out_specs=out_specs, check_vma=False
    )
```

profile of v0, /device:TPU:0, one launch (start us, length us, event | category | flops | bytes accessed | tf_op | source)
XLA Modules:
  0.0 813.7 jit_solution(3520903550146359245)
XLA Ops:
  7.2 0.7 broadcast_multiply_fusion
  7.9 0.8 eq.29
  8.6 0.8 eq.25
  9.4 0.1 mul.43
  9.5 0.1 copy.10
  9.6 0.2 fusion.9
  9.9 0.8 reshape.120
  10.6 0.2 fusion.11
  10.8 1.4 scatter_custom_fusion
  12.2 0.7 all_to_all.11
  13.0 11.1 %all-to-all-start = ((s32[128,1,4]{2,1,0:T(1,128)}), s32[128,1,4]{2,1,0:T(1,128)S(1)}, u32[]{:S(2)}, u32[]{:S(2)}) async-start(s32[128,1,4]{2,1,0:T(1,128)} %bitcast.5), calls=%async_computation.1 | async-start | bytes 131072 | tf_op jit(solution)/shard_map/all_to_all | solution.py:48
  24.1 0.7 slice.12
  24.8 36.6 %all_gather.3 = bf16[1024,256]{1,0:T(8,128)(2,1)S(1)} all-gather(bf16[8,256]{1,0:T(8,128)(2,1)S(1)} %slice.12), channel_id=1, replica_groups=mesh['index'=16,'query'=8] {'index','query'}, dimensions={0}, use_global_device_ids=true | all-gather | bytes 528384 | tf_op jit(solution)/shard_map/all_gather | solution.py:18
  61.4 9.7 %multiply_reduce_fusion = (f32[1024]{0:T(1024)S(1)}, f32[1024,4096]{1,0:T(8,128)}) fusion(bf16[1024,256]{1,0:T(8,128)(2,1)S(1)} %all_gather.3, bf16[4096,2048]{1,0:T(8,128)(2,1)} %param.5), kind=kOutput, calls=%fused_computation.4 | convolution fusion | flops 2155871232 | bytes 19402752 | tf_op jit(solution)/shard_map/dot_general | solution.py:17
  71.1 64.6 %pmax.7 = f32[1024]{0:T(1024)S(1)} all-reduce(f32[1024]{0:T(1024)S(1)} %get-tuple-element.5), channel_id=1, replica_groups=mesh['index'=16,'query'=8] {'index','query'}, use_global_device_ids=true, to_apply=%region_1.0 | all-reduce | flops 1024 | bytes 8192 | tf_op jit(solution)/shard_map/pmax | solution.py:25
  135.7 0.0 all-to-all-done
  135.7 0.1 reshape.102
  135.9 12.3 %gather_fusion = bf16[512,2048]{1,0:T(8,128)(2,1)S(1)} fusion(bf16[4096,2048]{1,0:T(8,128)(2,1)} %param.5, s32[1024]{0:T(1024)S(1)} %pad_clamp_fusion.1), kind=kCustom, calls=%fused_computation | custom fusion | bytes 4196352 | tf_op jit(solution)/shard_map/gather | solution.py:47
  148.2 2.2 reshape.101
  150.4 5.8 all-to-all-start.1
  156.2 0.3 reduce-scatter.2.cloned.1.call-start
  156.5 10.0 %fusion.2 = f32[1024,256]{1,0:T(8,128)} fusion(f32[1024,4096]{1,0:T(8,128)} %get-tuple-element.6, f32[1024]{0:T(1024)S(1)} %pmax.7, bf16[4096,2048]{1,0:T(8,128)(2,1)} %param.5), kind=kOutput, calls=%fused_computation.7 | convolution fusion | flops 2160066560 | bytes 19927040 | tf_op jit(solution)/shard_map/dot_general | solution.py:28
  166.5 0.0 copy-start.1
  166.5 0.0 reduce-scatter.2.cloned.1.call-update
  166.5 8.6 %fusion = f32[1024]{0:T(1024)S(1)} fusion(f32[1024,4096]{1,0:T(8,128)} %get-tuple-element.6, f32[1024]{0:T(1024)S(1)} %pmax.7), kind=kLoop, calls=%fused_computation.5 | loop fusion | flops 12581888 | bytes 16785408 | tf_op jit(solution)/shard_map/reduce_sum | solution.py:29
  175.2 68.0 %all-reduce = f32[1024]{0:T(1024)S(1)} all-reduce(f32[1024]{0:T(1024)S(1)} %fusion), channel_id=3, replica_groups=mesh['index'=16,'query'=8] {'index','query'}, use_global_device_ids=true, to_apply=%region_4.0.clone | all-reduce | flops 1024 | bytes 8192
  243.1 0.1 log_add_fusion
  243.2 0.0 copy-start
  243.2 0.0 all-to-all-done.1
  243.2 2.5 reshape.98
  245.8 1.4 gather_fusion.1
  247.2 0.0 copy-done.1
  247.2 0.4 fusion.13
  247.5 0.7 multiply_subtract_fusion
  248.2 557.3 %reduce-scatter.2.cloned.1.call-done = f32[8,256]{1,0:T(8,128)} async-done(((f32[1024,256]{1,0:T(8,128)}), f32[8,256]{1,0:T(8,128)}) %reduce-scatter.2.cloned.1.call-update) | async-done | bytes 8208 | tf_op jit(solution)/shard_map/reduce_scatter | solution.py:31
  805.5 1.4 broadcast_divide_fusion
  806.9 0.0 copy-done
  (10 shorter events, 0.1 us)
Async XLA Ops:
  13.0 122.7 %all-to-all-start = ((s32[128,1,4]{2,1,0:T(1,128)}), s32[128,1,4]{2,1,0:T(1,128)S(1)}, u32[]{:S(2)}, u32[]{:S(2)}) async-start(s32[128,1,4]{2,1,0:T(1,128)} %bitcast.5), calls=%async_computation.1 | async-start | bytes 131072 | tf_op jit(solution)/shard_map/all_to_all | solution.py:48
  150.4 92.8 %all-to-all-start.1 = ((bf16[128,4,2048]{2,1,0:T(4,128)(2,1)}), bf16[128,4,2048]{2,1,0:T(4,128)(2,1)}, u32[]{:S(2)}, u32[]{:S(2)}) async-start(bf16[128,4,2048]{2,1,0:T(4,128)(2,1)} %reshape.101), calls=%async_computation.2 | async-start | bytes 4194304 | tf_op jit(solution)/shard_map/all_to_all | solution.py:46
  156.2 649.3 %reduce-scatter.2.cloned.1.call-start = ((), (), s32[]{:S(2)}) async-start(), calls=%async_computation.3 | async-start | bytes 1056768 | tf_op jit(solution)/shard_map/reduce_scatter | solution.py:31
  166.5 80.7 %copy-start.1 = (bf16[8,2048]{1,0:T(8,128)(2,1)S(1)}, bf16[8,2048]{1,0:T(8,128)(2,1)}, u32[]{:S(2)}) copy-start(bf16[8,2048]{1,0:T(8,128)(2,1)} %param.4) | copy-start | bytes 98308
  243.2 563.7 %copy-start = (f32[8]{0:T(128)}, f32[8]{0:T(128)S(1)}, u32[]{:S(2)}) copy-start(f32[8]{0:T(128)S(1)} %get-tuple-element.3) | copy-start | bytes 100
Sparse Core Ops, SparseCore 0:
  166.6 638.8 reduce-scatter.1
where the time goes:
time: 815 us; the launch traced here: 814 us
  waiting for transfers between devices  557 us (68%)
  blocking collectives  169 us (21%)
  local copies, waits for them, and re-layouts  23.9 us (3%)
  matrix products  20.1 us (2%)
  starting transfers between devices  17.2 us (2%)
  between operations  14.2 us (2%)
  other arithmetic  11.9 us (1%)
    reduce_scatter x1, waiting for transfers between devices, on_device(): lax.psum_scatter(parts, ('index', 'query'), scatter_dimension=0, tiled=True)  557 us
    unnamed x1, blocking collectives  68 us
    pmax x1, blocking collectives, on_device(): top = lax.pmax(jnp.max(logits, axis=1), ('index', 'query'))  64.6 us
    all_gather x1, blocking collectives, on_device(): lax.all_gather(queries[:, :PREFIX], ('index', 'query'), axis=0, tiled=True)  36.6 us
  transfers between devices with their start and end apart: 3, of which 1 were waited for; matrix products, arithmetic and copies ran while one was open for 4% of the time, Pallas kernels for 0%

commit v1 on v0

v1 whole, which is shorter than its diff:
```python
import functools
import math

import jax
import jax.numpy as jnp
from jax import lax
from jax.experimental import pallas as pl
from jax.experimental.pallas import tpu as pltpu
from jax.sharding import PartitionSpec as P

PREFIX = 256
LANES = 128
QB = 8
SLOTS = 4
F32 = jnp.float32
BF16 = jnp.bfloat16
ORDERS = ((1, 0, 2), (0, 2, 1), (2, 1, 0))
NT = (((1,), (1,)), ((), ()))
M_LANE = 127
L_LANE = 96
F_LANE = 64


def lane_of(rows):
    return lax.broadcasted_iota(jnp.int32, (rows, LANES), 1)


def merge(part, blocks):
    lane = lane_of(blocks[0].shape[0])
    maxima = [b[:, M_LANE:] for b in blocks]
    top = functools.reduce(jnp.maximum, maxima)
    total = None
    for b, m in zip(blocks, maxima):
        s = jnp.broadcast_to(jnp.exp2(m - top), b.shape)
        if part == 2:
            s = jnp.where((lane >= F_LANE) & (lane < L_LANE), 1.0, s)
        total = b * s if total is None else total + b * s
    return jnp.where(lane == M_LANE, top, total)


def kernel(
    dims,
    col0,
    q_ref,
    slab_ref,
    own_ref,
    row_ref,
    pooled_ref,
    lse_ref,
    margin_ref,
    slab_v,
    x_buf,
    f0,
    f1,
    f2,
    sel_buf,
    hot,
    rows_buf,
    logits,
    pay,
    got0,
    mid0,
    got1,
    mid1,
    got2,
    mid2,
    got3,
    lsem,
    xs,
    xr,
    fs,
    fr,
    rs,
    rr,
):
    width = q_ref.shape[1]
    r_dev = slab_ref.shape[0]
    ii, qq = lax.axis_index("index"), lax.axis_index("query")
    coord = (lax.div(ii, dims[1]), lax.rem(ii, dims[1]), lax.div(qq, 2))
    core = lax.rem(qq, 2)
    me = ii * (dims[2] * 2) + qq
    chunk = dims[1] * dims[2] * 2 * QB
    k_count = row_ref.shape[1]
    f_bufs = (f0, f1, f2)

    def device(at, c):
        return (at[0] * dims[1] + at[1], at[2] * 2 + c)

    def peer(axis, k):
        at = list(coord)
        at[axis] = lax.rem(coord[axis] + k, dims[axis])
        return tuple(at)

    sibling = device(coord, 1 - core)

    pre_copy = pltpu.make_async_copy(
        slab_ref.at[:, pl.ds(0, PREFIX)], slab_v.at[:, pl.ds(0, PREFIX)], lsem.at[0]
    )
    rest_copy = pltpu.make_async_copy(
        slab_ref.at[:, pl.ds(PREFIX, width - PREFIX)],
        slab_v.at[:, pl.ds(PREFIX, width - PREFIX)],
        lsem.at[1],
    )
    pre_copy.start()
    rest_copy.start()

    barrier = pltpu.get_barrier_semaphore()
    n_peers = 1
    pl.semaphore_signal(barrier, inc=1, device_id=sibling, device_id_type=pl.DeviceIdType.MESH)
    for axis in range(3):
        for k in range(1, dims[axis]):
            n_peers += 1
            pl.semaphore_signal(
                barrier, inc=1, device_id=device(peer(axis, k), core), device_id_type=pl.DeviceIdType.MESH
            )

    here = coord + (core,)
    x_buf[(0,) + here] = q_ref[:, 0:LANES]
    x_buf[(1,) + here] = q_ref[:, LANES:PREFIX]
    row = row_ref[...]
    numbers = jnp.concatenate(
        [
            own_ref[...].astype(F32),
            lax.shift_right_logical(row, 6).astype(F32),
            (row & 63).astype(F32),
            jnp.zeros((QB, LANES - 3 * row.shape[1]), F32),
        ],
        axis=1,
    )
    x_buf[(2,) + here] = numbers.astype(BF16)
    for p in range(3):
        f_bufs[p][here] = q_ref[:, col0[p] : col0[p + 1]]
    pl.semaphore_wait(barrier, n_peers)

    def copy(src, dst, ssem, rsem, target):
        return pltpu.make_async_remote_copy(
            src_ref=src,
            dst_ref=dst,
            send_sem=ssem,
            recv_sem=rsem,
            device_id=target,
            device_id_type=pl.DeviceIdType.MESH,
        )

    def gather_step(bufs, ssem, rsem, phase):
        started = []
        for p in range(3):
            if phase == 3:
                block = bufs[p].at[:, :, :, core]
                targets = [sibling]
            else:
                done = ORDERS[p][:phase]
                where = tuple(slice(None) if a in done else coord[a] for a in range(3))
                block = bufs[p].at[where + (core,)]
                axis = ORDERS[p][phase]
                targets = [device(peer(axis, k), core) for k in range(1, dims[axis])]
            for k, target in enumerate(targets):
                at = (p * 4 + phase) * 3 + k
                c = copy(block, block, ssem.at[at], rsem.at[at], target)
                c.start()
                started.append(c)
        return started

    x_bufs = [x_buf.at[p] for p in range(3)]
    sent = []

    def arrived(copies):
        for c in copies:
            c.wait_recv()
        sent.extend(copies)

    x_now = gather_step(x_bufs, xs, xr, 0)
    f_now = gather_step(f_bufs, fs, fr, 0)
    arrived(x_now)
    x_now = gather_step(x_bufs, xs, xr, 1)
    arrived(f_now)
    arrived(x_now)
    x_now = gather_step(x_bufs, xs, xr, 2)
    f_now = gather_step(f_bufs, fs, fr, 1)
    arrived(x_now)
    x_now = gather_step(x_bufs, xs, xr, 3)
    arrived(f_now)
    f_now = gather_step(f_bufs, fs, fr, 2)
    arrived(x_now)

    def x_part(p, y):
        return x_buf[p, y].astype(F32).reshape(chunk, LANES)

    me_f = me.astype(F32)
    n_slot = chunk // QB * SLOTS

    @pl.loop(0, dims[0])
    def _(y):
        numbers = x_part(2, y)
        lane = lane_of(chunk)
        hit = (numbers == me_f) & (lane < k_count)
        high = pltpu.roll(numbers, LANES - k_count, 1)
        low = pltpu.roll(numbers, LANES - 2 * k_count, 1)
        any_hit = jnp.sum(jnp.where(hit, 1.0, 0.0), axis=1, keepdims=True)
        high = jnp.sum(jnp.where(hit, high, 0.0), axis=1, keepdims=True)
        low = jnp.sum(jnp.where(hit, low, 0.0), axis=1, keepdims=True)
        qi = lax.broadcasted_iota(jnp.int32, (chunk, chunk), 0)
        qj = lax.broadcasted_iota(jnp.int32, (chunk, chunk), 1)
        before = jnp.where(((qi >> 3) == (qj >> 3)) & (qj < qi), 1.0, 0.0).astype(BF16)
        rank = jnp.dot(
            before,
            jnp.broadcast_to(any_hit, (chunk, LANES)).astype(BF16),
            preferred_element_type=F32,
        )[:, 0:1]
        rank = jnp.where(any_hit > 0.0, rank, -1.0)
        q_of = lax.broadcasted_iota(jnp.int32, (chunk, n_slot), 0)
        s_of = lax.broadcasted_iota(jnp.int32, (chunk, n_slot), 1)
        sel = jnp.where(
            ((q_of >> 3) == (s_of >> 2)) & (rank == (s_of & 3).astype(F32)), 1.0, 0.0
        )
        sel_buf[y] = sel
        picked = jnp.dot(
            sel.T.astype(BF16),
            jnp.where(lane < 64, high, low).astype(BF16),
            preferred_element_type=F32,
        )
        row_of = (picked[:, 0:1] * 64.0 + picked[:, 64:65]).astype(jnp.int32)
        rows = pl.ds(pl.multiple_of(y * n_slot, n_slot), n_slot)
        for t in range(r_dev // 512):
            r = lax.broadcasted_iota(jnp.int32, (n_slot, 512), 1) + t * 512
            hot[rows, t * 512 : (t + 1) * 512] = jnp.where(r == row_of, 1.0, 0.0).astype(BF16)

    pre_copy.wait()
    rest_copy.wait()

    @pl.loop(0, width // 256)
    def _(n):
        cols = pl.ds(pl.multiple_of(n * 256, 256), 256)
        rows_buf[:, cols] = jnp.dot(hot[...], slab_v[:, cols], preferred_element_type=F32).astype(BF16)

    arrived(f_now)
    f_now = gather_step(f_bufs, fs, fr, 3)

    factor = PREFIX ** (-0.5) * math.log2(math.e)
    tile = 512

    @pl.loop(0, dims[0])
    def _(y):
        q = jnp.concatenate([x_part(0, y), x_part(1, y)], axis=1).astype(BF16)
        most = jnp.full((chunk, LANES), -jnp.inf, F32)
        for t in range(r_dev // tile):
            s = lax.dot_general(
                q, slab_v[t * tile : (t + 1) * tile, 0:PREFIX], NT, preferred_element_type=F32
            )
            logits[:, t * tile : (t + 1) * tile] = s
            for u in range(tile // LANES):
                most = jnp.maximum(most, s[:, u * LANES : (u + 1) * LANES])
        top = jnp.max(most, axis=1, keepdims=True) * factor
        total = jnp.zeros((chunk, LANES), F32)
        acc = jnp.zeros((chunk, PREFIX), F32)
        for t in range(r_dev // tile):
            w = jnp.exp2(logits[:, t * tile : (t + 1) * tile] * factor - top)
            for u in range(tile // LANES):
                total = total + w[:, u * LANES : (u + 1) * LANES]
            acc = acc + jnp.dot(
                w.astype(BF16), slab_v[t * tile : (t + 1) * tile, 0:PREFIX], preferred_element_type=F32
            )
        total = jnp.sum(total, axis=1, keepdims=True)
        lane = lane_of(chunk)
        p0, p1 = acc[:, :LANES], acc[:, LANES:]
        r1 = pltpu.roll(p1, 32, 1)
        shape = (dims[1], dims[2], 2, QB, LANES)
        pay[0, y] = jnp.where(lane == M_LANE, top, p0).reshape(shape)
        b = jnp.where(lane < 32, pltpu.roll(p0, 32, 1), r1)
        pay[1, y] = jnp.where(lane == M_LANE, top, b).reshape(shape)
        c = jnp.where(lane < F_LANE, pltpu.roll(p1, 64, 1), 0.0)
        c = jnp.where(lane == L_LANE, total, c)
        pay[2, y] = jnp.where(lane == M_LANE, top, c).reshape(shape)

    arrived(f_now)

    @pl.loop(0, dims[0])
    def _(y):
        rows = pl.ds(pl.multiple_of(y * n_slot, n_slot), n_slot)
        q = jnp.concatenate([x_part(0, y), x_part(1, y)], axis=1).astype(BF16)
        scores = lax.dot_general(q, rows_buf[rows, 0:PREFIX], NT, preferred_element_type=F32)
        for p in range(3):
            q = f_bufs[p][y].astype(F32).reshape(chunk, col0[p + 1] - col0[p]).astype(BF16)
            scores = scores + lax.dot_general(
                q, rows_buf[rows, col0[p] : col0[p + 1]], NT, preferred_element_type=F32
            )
        full = jnp.sum(scores * sel_buf[y], axis=1, keepdims=True)
        lane = lane_of(chunk)
        mine = jnp.where((x_part(2, y) == me_f) & (lane < k_count), full, 0.0)
        mine = pltpu.roll(mine, F_LANE, 1)
        pay[2, y] = pay[2, y] + mine.reshape(dims[1], dims[2], 2, QB, LANES)

    def at_part(p):
        return p * 4 * 3

    now = []
    for p in range(3):
        at = at_part(p)
        c = copy(pay.at[p, :, :, :, 1 - core], got0.at[p], rs.at[at], rr.at[at], sibling)
        c.start()
        now.append(c)
    flat0 = (dims[0] * dims[1] * dims[2] * QB, LANES)
    for p in range(3):
        now[p].wait_recv()
        a = pay[p, :, :, :, core].reshape(flat0)
        mid0[p] = merge(p, [a, got0[p].reshape(flat0)]).reshape(dims + (QB, LANES))
        sent.append(now[p])

        axis = ORDERS[p][0]
        started = []
        for k in range(1, dims[axis]):
            where = tuple(peer(axis, k)[a] if a == axis else slice(None) for a in range(3))
            at = at_part(p) + 3 + k - 1
            c = copy(mid0.at[(p,) + where], got1.at[p, k - 1], rs.at[at], rr.at[at], device(peer(axis, k), core))
            c.start()
            started.append(c)
        now[p] = started

    def pick(value_ref, axis, index):
        where = tuple(index if a == axis else slice(None) for a in range(3))
        return where

    for p in range(3):
        arrived(now[p])
        first, second, third = ORDERS[p]
        n1 = [dims[a] for a in range(3) if a != first]
        flat1 = (n1[0] * n1[1] * QB, LANES)
        own = mid0[(p,) + pick(mid0, first, coord[first])].reshape(flat1)
        blocks = [own] + [got1[p, k - 1].reshape(flat1) for k in range(1, dims[first])]
        mid1[p] = merge(p, blocks).reshape(n1[0], n1[1], QB, LANES)
        left = [a for a in range(3) if a != first]
        started = []
        for k in range(1, dims[second]):
            to = peer(second, k)
            where = tuple(to[a] if a == second else slice(None) for a in left)
            at = at_part(p) + 6 + k - 1
            c = copy(mid1.at[(p,) + where], got2.at[p, k - 1], rs.at[at], rr.at[at], device(to, core))
            c.start()
            started.append(c)
        now[p] = started

    for p in range(3):
        arrived(now[p])
        first, second, third = ORDERS[p]
        left = [a for a in range(3) if a != first]
        flat2 = (dims[third] * QB, LANES)
        where = tuple(coord[a] if a == second else slice(None) for a in left)
        own = mid1[(p,) + where].reshape(flat2)
        blocks = [own] + [got2[p, k - 1].reshape(flat2) for k in range(1, dims[second])]
        mid2[p] = merge(p, blocks).reshape(dims[third], QB, LANES)
        started = []
        for k in range(1, dims[third]):
            to = peer(third, k)
            at = at_part(p) + 9 + k - 1
            c = copy(mid2.at[p, to[third]], got3.at[p, k - 1], rs.at[at], rr.at[at], device(to, core))
            c.start()
            started.append(c)
        now[p] = started

    out = []
    for p in range(3):
        arrived(now[p])
        third = ORDERS[p][2]
        own = mid2[p, coord[third]]
        out.append(merge(p, [own] + [got3[p, k - 1] for k in range(1, dims[third])]))

    lane = lane_of(QB)
    a, b, c = out
    total = c[:, L_LANE : L_LANE + 1]
    top = c[:, M_LANE:]
    b_back = pltpu.roll(b, 96, 1)
    pooled_ref[:, 0:LANES] = jnp.where(lane < 96, a, b_back) / total
    pooled_ref[:, LANES:PREFIX] = jnp.where(lane < 64, b_back, pltpu.roll(c, 64, 1)) / total
    lse = top * math.log(2.0) + jnp.log(total)
    lse_ref[...] = lse
    full = pltpu.roll(c, LANES - F_LANE, 1) * width ** (-0.5)
    margin_ref[...] = (full - lse)[:, : margin_ref.shape[1]]

    for c in sent:
        c.wait_send()


def make(mesh, dims):
    def on_device(queries, slab, cand_owner, cand_row):
        width = queries.shape[1]
        r_dev = slab.shape[0]
        k_count = cand_owner.shape[1]
        tiles = (width - PREFIX) // LANES
        n0 = -(-tiles // 3)
        n1 = -(-(tiles - n0) // 2)
        col0 = (PREFIX, PREFIX + n0 * LANES, PREFIX + (n0 + n1) * LANES, width)
        n_chunk = dims[1] * dims[2] * 2 * QB
        n_slot = n_chunk // QB * SLOTS
        side = max(dims)
        vmem = pltpu.VMEM
        dma = pltpu.SemaphoreType.DMA
        spec = pl.BlockSpec(memory_space=pltpu.VMEM)
        pooled, lse, margin = pl.pallas_call(
            functools.partial(kernel, dims, col0),
            out_shape=(
                jax.ShapeDtypeStruct((QB, PREFIX), F32),
                jax.ShapeDtypeStruct((QB, 1), F32),
                jax.ShapeDtypeStruct((QB, k_count), F32),
            ),
            in_specs=[spec, pl.BlockSpec(memory_space=pl.ANY), spec, spec],
            out_specs=(spec, spec, spec),
            scratch_shapes=[
                vmem((r_dev, width), BF16),
                vmem((3,) + dims + (2, QB, LANES), BF16),
                vmem(dims + (2, QB, col0[1] - col0[0]), BF16),
                vmem(dims + (2, QB, col0[2] - col0[1]), BF16),
                vmem(dims + (2, QB, col0[3] - col0[2]), BF16),
                vmem((dims[0], n_chunk, n_slot), F32),
                vmem((dims[0] * n_slot, r_dev), BF16),
                vmem((dims[0] * n_slot, width), BF16),
                vmem((n_chunk, r_dev), F32),
                vmem((3,) + dims + (2, QB, LANES), F32),
                vmem((3,) + dims + (QB, LANES), F32),
                vmem((3,) + dims + (QB, LANES), F32),
                vmem((3, side - 1, side, side, QB, LANES), F32),
                vmem((3, side, side, QB, LANES), F32),
                vmem((3, side - 1, side, QB, LANES), F32),
                vmem((3, side, QB, LANES), F32),
                vmem((3, side - 1, QB, LANES), F32),
                dma((2,)),
                dma((36,)),
                dma((36,)),
                dma((36,)),
                dma((36,)),
                dma((36,)),
                dma((36,)),
            ],
            compiler_params=pltpu.CompilerParams(
                collective_id=0, has_side_effects=True, vmem_limit_bytes=56 * 2**20
            ),
        )(queries, slab, cand_owner, cand_row)
        return pooled, lse.reshape(QB), margin

    both = ("index", "query")
    return jax.shard_map(
        on_device,
        mesh=mesh,
        in_specs=(P(both, None),) * 4,
        out_specs=(P(both, None), P(both), P(both, None)),
        check_vma=False,
    )


def solution(mesh):
    side = math.isqrt(mesh.shape["index"])
    return make(mesh, (side, side, mesh.shape["query"] // 2))
```

time: 815 us -> 72 us (0.09)
  waiting for transfers between devices: 557 us -> 0 us
  blocking collectives: 169 us -> 0 us
  Pallas kernels: 0 us -> 67.3 us
  local copies, waits for them, and re-layouts: 23.9 us -> 2.56 us
  matrix products: 20.1 us -> 0 us
  starting transfers between devices: 17.2 us -> 0 us
  between operations: 14.2 us -> 0.64 us
  other arithmetic: 11.9 us -> 1.3 us
    reduce_scatter x1 -> x0, waiting for transfers between devices: 557 us -> none  [on_device(): lax.psum_scatter(parts, ('index', 'query'), scatter_dimension=0, tiled=True)]
    unnamed x1 -> x0, blocking collectives: 68 us -> none
    pallas_call x0 -> x1, Pallas kernels: none -> 67.3 us  [on_device(): pl.pallas_call(functools.partial(kernel, dims, col0), out_shape=(jax.Shap...]
    pmax x1 -> x0, blocking collectives: 64.6 us -> none  [on_device(): top = lax.pmax(jnp.max(logits, axis=1), ('index', 'query'))]
    all_gather x1 -> x0, blocking collectives: 36.6 us -> none  [on_device(): lax.all_gather(queries[:, :PREFIX], ('index', 'query'), axis=0, tiled=True)]
    dot_general x3 -> x0, matrix products: 20.1 us -> none  [the longest x1 10 us: on_device(): jnp.dot(weights.astype(jnp.bfloat16), prefix_keys, preferred_element_type...]
    all_to_all x2 -> x0, starting transfers between devices: 16.9 us -> none  [the longest x1 11.1 us: on_device(): lax.all_to_all(request.reshape(owners, capacity), ('index', 'query'), spl...]
    gather x3 -> x0, local copies, waits for them, and re-layouts: 15.9 us -> none  [the longest x2 14.6 us: on_device(): slab[lax.all_to_all(request.reshape(owners, capacity), ('index', 'query')...]
  transfers between devices with their start and end apart: 3 -> 0, of which waited for: 1 -> 0; matrix products, arithmetic and copies ran while one was open for 4% -> 0% of each run, Pallas kernels for 0% -> 0%
where the time goes in v1:
time: 72 us; the launch traced here: 71.8 us
  Pallas kernels  67.3 us (93%)
  local copies, waits for them, and re-layouts  2.56 us (4%)
  other arithmetic  1.3 us (2%)
    pallas_call x1, Pallas kernels, on_device(): pl.pallas_call(functools.partial(kernel, dims, col0), out_shape=(jax.Shap...  67.3 us
    unnamed x2, local copies, waits for them, and re-layouts  2.56 us

profile of v1, /device:TPU:0, one launch (start us, length us, event | category | flops | bytes accessed | tf_op | source)
XLA Modules:
  0.0 71.8 jit_solution(10698924886461413891)
XLA Ops:
  0.6 67.3 %shard_map.67 = (f32[8,256]{1,0:T(8,128)}, f32[8,1]{1,0:T(8,128)}, f32[8,32]{1,0:T(8,128)}) custom-call(bf16[8,2048]{1,0:T(8,128)(2,1)} %q_ref.1, bf16[4096,2048]{1,0:T(8,128)(2,1)} %slab_ref.1, s32[8,32]{1,0:T(8,128)} %own_ref.1, s32[8,32]{1,0:T(8,128)} %row_ref.1), custom_call_target="tpu_custom_call" | custom-call | tf_op jit(solution)/shard_map/pallas_call | solution.py:398
  67.9 1.3 %reduce = f32[8]{0:T(128)} reduce(f32[8,1]{1,0:T(8,128)} %get-tuple-element.7, f32[]{:T(128)} %constant.3), dimensions={1}, to_apply=%get-tuple-element.7.reduce_sub_computation | reduce | bytes 68 | tf_op jit(solution)/shard_map/pallas_call | solution.py:398
  69.2 1.3 %copy.9 = f32[8,256]{1,0:T(8,128)} copy(f32[8,256]{1,0:T(8,128)} %get-tuple-element.12) | data formatting | bytes 16384
  70.5 1.3 %copy.10 = f32[8,32]{1,0:T(8,128)} copy(f32[8,32]{1,0:T(8,128)} %get-tuple-element.14) | data formatting | bytes 2048

commit v2 on v1

v2 whole, which is shorter than its diff:
```python
import functools
import math

import jax
import jax.numpy as jnp
from jax import lax
from jax.experimental import pallas as pl
from jax.experimental.pallas import tpu as pltpu
from jax.sharding import PartitionSpec as P

PREFIX = 256
LANES = 128
QB = 8
SLOTS = 4
F32 = jnp.float32
BF16 = jnp.bfloat16
ORDERS = ((1, 0, 2), (0, 2, 1), (2, 1, 0))
NT = (((1,), (1,)), ((), ()))
M_LANE = 127
L_LANE = 96
F_LANE = 64


def lane_of(rows):
    return lax.broadcasted_iota(jnp.int32, (rows, LANES), 1)


def merge(part, blocks):
    lane = lane_of(blocks[0].shape[0])
    maxima = [b[:, M_LANE:] for b in blocks]
    top = functools.reduce(jnp.maximum, maxima)
    total = None
    for b, m in zip(blocks, maxima):
        s = jnp.broadcast_to(jnp.exp2(m - top), b.shape)
        if part == 2:
            s = jnp.where((lane >= F_LANE) & (lane < L_LANE), 1.0, s)
        total = b * s if total is None else total + b * s
    return jnp.where(lane == M_LANE, top, total)


def kernel(
    dims,
    col0,
    q_ref,
    slab_ref,
    own_ref,
    row_ref,
    out_ref,
    slab_v,
    x_buf,
    f0,
    f1,
    f2,
    sel_buf,
    hot,
    rows_buf,
    logits,
    pay,
    got0,
    mid0,
    got1,
    mid1,
    got2,
    mid2,
    got3,
    lsem,
    xs,
    xr,
    fs,
    fr,
    s0,
    r0,
    rs,
    rr,
):
    width = q_ref.shape[1]
    r_dev = slab_ref.shape[0]
    ii, qq = lax.axis_index("index"), lax.axis_index("query")
    coord = (lax.div(ii, dims[1]), lax.rem(ii, dims[1]), lax.div(qq, 2))
    core = lax.rem(qq, 2)
    me_f = (ii * (dims[2] * 2) + qq).astype(F32)
    n = dims[0]
    pairs = n // 2
    k_count = row_ref.shape[1]
    box = (2, n, n, QB, LANES)
    chunk = 2 * n * n * QB
    n_slot = chunk // QB * SLOTS
    f_bufs = (f0, f1, f2)
    x_bufs = [x_buf.at[p] for p in range(3)]

    def device(at, c):
        return (at[0] * n + at[1], at[2] * 2 + c)

    def peer(axis, k):
        at = list(coord)
        at[axis] = lax.rem(coord[axis] + k, n)
        return tuple(at)

    sibling = device(coord, 1 - core)

    pre_copy = pltpu.make_async_copy(
        slab_ref.at[:, pl.ds(0, PREFIX)], slab_v.at[:, pl.ds(0, PREFIX)], lsem.at[0]
    )
    rest_copy = pltpu.make_async_copy(
        slab_ref.at[:, pl.ds(PREFIX, width - PREFIX)],
        slab_v.at[:, pl.ds(PREFIX, width - PREFIX)],
        lsem.at[1],
    )

    barrier = pltpu.get_barrier_semaphore()
    pl.semaphore_signal(barrier, inc=1, device_id=sibling, device_id_type=pl.DeviceIdType.MESH)
    for axis in range(3):
        for k in range(1, n):
            pl.semaphore_signal(
                barrier, inc=1, device_id=device(peer(axis, k), core), device_id_type=pl.DeviceIdType.MESH
            )
    pre_copy.start()
    rest_copy.start()

    here = coord + (core,)
    x_buf[(0,) + here] = q_ref[:, 0:LANES]
    x_buf[(1,) + here] = q_ref[:, LANES:PREFIX]
    row = row_ref[...]
    numbers = jnp.concatenate(
        [
            own_ref[...].astype(F32),
            lax.shift_right_logical(row, 6).astype(F32),
            (row & 63).astype(F32),
            jnp.zeros((QB, LANES - 3 * k_count), F32),
        ],
        axis=1,
    )
    x_buf[(2,) + here] = numbers.astype(BF16)
    for p in range(3):
        f_bufs[p][here] = q_ref[:, col0[p] : col0[p + 1]]
    pl.semaphore_wait(barrier, 1 + 3 * (n - 1))

    def send(src, dst, ssem, rsem, target):
        pltpu.make_async_remote_copy(
            src_ref=src,
            dst_ref=dst,
            send_sem=ssem,
            recv_sem=rsem,
            device_id=target,
            device_id_type=pl.DeviceIdType.MESH,
        ).start()

    def wait_bytes(ref, sem):
        pltpu.make_async_copy(ref, ref, sem).wait()

    def phase_box(phase):
        if phase == 3:
            return (slice(None),) * 3 + (0,)
        return (slice(0, n - 1),) + (slice(None),) * phase + (0,) * (2 - phase) + (0,)

    def gather_start(bufs, ssem_of, rsem, phase, p):
        if phase == 3:
            block = bufs[p].at[:, :, :, core]
            targets = [sibling]
        else:
            done = ORDERS[p][:phase]
            where = tuple(slice(None) if a in done else coord[a] for a in range(3))
            block = bufs[p].at[where + (core,)]
            axis = ORDERS[p][phase]
            targets = [device(peer(axis, k), core) for k in range(1, n)]
        for target in targets:
            send(block, block, ssem_of(p, phase), rsem.at[p * 4 + phase], target)

    def x_ssem(p, phase):
        return xs.at[phase]

    def f_ssem(p, phase):
        return fs.at[p * 4 + phase]

    def x_start(phase):
        for p in range(3):
            gather_start(x_bufs, x_ssem, xr, phase, p)

    def f_start(phase):
        for p in range(3):
            gather_start(f_bufs, f_ssem, fr, phase, p)

    def x_step(phase):
        for p in range(3):
            wait_bytes(x_bufs[p].at[phase_box(phase)], xr.at[p * 4 + phase])
            if phase < 3:
                gather_start(x_bufs, x_ssem, xr, phase + 1, p)

    def f_step(phase):
        for p in range(3):
            wait_bytes(f_bufs[p].at[phase_box(phase)], fr.at[p * 4 + phase])
            if phase < 3:
                gather_start(f_bufs, f_ssem, fr, phase + 1, p)

    x_start(0)
    f_start(0)
    x_step(0)
    x_step(1)
    f_step(0)
    x_step(2)
    f_step(1)

    def part_of(buf, t, c):
        v = buf[pl.ds(2 * t, 2), :, :, c]
        return v.astype(F32).reshape(chunk, v.shape[-1])

    def index(j, t, c):
        numbers = part_of(x_bufs[2], t, c)
        lane = lane_of(chunk)
        hit = (numbers == me_f) & (lane < k_count)
        high = pltpu.roll(numbers, LANES - k_count, 1)
        low = pltpu.roll(numbers, LANES - 2 * k_count, 1)
        any_hit = jnp.sum(jnp.where(hit, 1.0, 0.0), axis=1, keepdims=True)
        high = jnp.sum(jnp.where(hit, high, 0.0), axis=1, keepdims=True)
        low = jnp.sum(jnp.where(hit, low, 0.0), axis=1, keepdims=True)
        qi = lax.broadcasted_iota(jnp.int32, (chunk, chunk), 0)
        qj = lax.broadcasted_iota(jnp.int32, (chunk, chunk), 1)
        before = jnp.where(((qi >> 3) == (qj >> 3)) & (qj < qi), 1.0, 0.0).astype(BF16)
        rank = jnp.dot(
            before,
            jnp.broadcast_to(any_hit, (chunk, LANES)).astype(BF16),
            preferred_element_type=F32,
        )[:, 0:1]
        rank = jnp.where(any_hit > 0.0, rank, -1.0)
        q_of = lax.broadcasted_iota(jnp.int32, (chunk, n_slot), 0)
        s_of = lax.broadcasted_iota(jnp.int32, (chunk, n_slot), 1)
        sel = jnp.where(
            ((q_of >> 3) == (s_of >> 2)) & (rank == (s_of & 3).astype(F32)), 1.0, 0.0
        )
        sel_buf[j] = sel
        picked = jnp.dot(
            sel.T.astype(BF16),
            jnp.where(lane < 64, high, low).astype(BF16),
            preferred_element_type=F32,
        )
        row_of = (picked[:, 0:1] * 64.0 + picked[:, 64:65]).astype(jnp.int32)
        rows = pl.ds(pl.multiple_of(j * n_slot, n_slot), n_slot)
        for u in range(r_dev // 512):
            r = lax.broadcasted_iota(jnp.int32, (n_slot, 512), 1) + u * 512
            hot[rows, u * 512 : (u + 1) * 512] = jnp.where(r == row_of, 1.0, 0.0).astype(BF16)

    @pl.loop(0, pairs)
    def _(t):
        index(t, t, core)

    x_step(3)

    @pl.loop(0, pairs)
    def _(t):
        index(pairs + t, t, 1 - core)

    pre_copy.wait()
    rest_copy.wait()

    def pick_rows(i):
        cols = pl.ds(pl.multiple_of(i * 256, 256), 256)
        rows_buf[:, cols] = jnp.dot(hot[...], slab_v[:, cols], preferred_element_type=F32).astype(BF16)

    half = width // 512

    @pl.loop(0, half)
    def _(i):
        pick_rows(i)

    f_step(2)

    @pl.loop(half, width // 256)
    def _(i):
        pick_rows(i)

    f_step(3)

    factor = PREFIX ** (-0.5) * math.log2(math.e)
    tile = 512

    def score(j, t, c):
        q = jnp.concatenate([part_of(x_bufs[0], t, c), part_of(x_bufs[1], t, c)], axis=1).astype(BF16)
        most = jnp.full((chunk, LANES), -jnp.inf, F32)
        for u in range(r_dev // tile):
            s = lax.dot_general(
                q, slab_v[u * tile : (u + 1) * tile, 0:PREFIX], NT, preferred_element_type=F32
            )
            logits[:, u * tile : (u + 1) * tile] = s
            for v in range(tile // LANES):
                most = jnp.maximum(most, s[:, v * LANES : (v + 1) * LANES])
        top = jnp.max(most, axis=1, keepdims=True) * factor
        total = jnp.zeros((chunk, LANES), F32)
        acc = jnp.zeros((chunk, PREFIX), F32)
        for u in range(r_dev // tile):
            w = jnp.exp2(logits[:, u * tile : (u + 1) * tile] * factor - top)
            for v in range(tile // LANES):
                total = total + w[:, v * LANES : (v + 1) * LANES]
            acc = acc + jnp.dot(
                w.astype(BF16), slab_v[u * tile : (u + 1) * tile, 0:PREFIX], preferred_element_type=F32
            )
        total = jnp.sum(total, axis=1, keepdims=True)

        rows = pl.ds(pl.multiple_of(j * n_slot, n_slot), n_slot)
        scores = lax.dot_general(q, rows_buf[rows, 0:PREFIX], NT, preferred_element_type=F32)
        for p in range(3):
            scores = scores + lax.dot_general(
                part_of(f_bufs[p], t, c).astype(BF16),
                rows_buf[rows, col0[p] : col0[p + 1]],
                NT,
                preferred_element_type=F32,
            )
        full = jnp.sum(scores * sel_buf[j], axis=1, keepdims=True)

        lane = lane_of(chunk)
        full = jnp.where((part_of(x_bufs[2], t, c) == me_f) & (lane < k_count), full, 0.0)
        p0, p1 = acc[:, :LANES], acc[:, LANES:]
        b = jnp.where(lane < 32, pltpu.roll(p0, 32, 1), pltpu.roll(p1, 32, 1))
        c = jnp.where(lane < F_LANE, pltpu.roll(p1, 64, 1), pltpu.roll(full, F_LANE, 1))
        c = jnp.where(lane == L_LANE, total, c)
        return [jnp.where(lane == M_LANE, top, v) for v in (p0, b, c)]

    @pl.loop(0, pairs)
    def _(t):
        for p, v in enumerate(score(pairs + t, t, 1 - core)):
            pay[t, p] = v.reshape(box)
        send(pay.at[t], got0.at[t], s0.at[t], r0.at[t], sibling)

    @pl.loop(0, pairs)
    def _(t):
        mine = score(t, t, core)
        wait_bytes(got0.at[t], r0.at[t])
        for p in range(3):
            both = merge(p, [mine[p], got0[t, p].reshape(chunk, LANES)])
            mid0[p, pl.ds(2 * t, 2)] = both.reshape(box)

    def at_axis(axes, axis, index):
        return tuple(index if a == axis else slice(None) for a in axes)

    for p in range(3):
        axis = ORDERS[p][0]
        for k in range(1, n):
            to = peer(axis, k)
            send(mid0.at[(p,) + at_axis(range(3), axis, to[axis])], got1.at[p, k - 1], rs.at[0], rr.at[p], device(to, core))

    flat1 = (n * n * QB, LANES)
    for p in range(3):
        wait_bytes(got1.at[p], rr.at[p])
        first, second, third = ORDERS[p]
        own = mid0[(p,) + at_axis(range(3), first, coord[first])].reshape(flat1)
        blocks = [own] + [got1[p, k - 1].reshape(flat1) for k in range(1, n)]
        mid1[p] = merge(p, blocks).reshape(n, n, QB, LANES)
        left = [a for a in range(3) if a != first]
        for k in range(1, n):
            to = peer(second, k)
            send(mid1.at[(p,) + at_axis(left, second, to[second])], got2.at[p, k - 1], rs.at[1], rr.at[3 + p], device(to, core))

    flat2 = (n * QB, LANES)
    for p in range(3):
        wait_bytes(got2.at[p], rr.at[3 + p])
        first, second, third = ORDERS[p]
        left = [a for a in range(3) if a != first]
        own = mid1[(p,) + at_axis(left, second, coord[second])].reshape(flat2)
        blocks = [own] + [got2[p, k - 1].reshape(flat2) for k in range(1, n)]
        mid2[p] = merge(p, blocks).reshape(n, QB, LANES)
        for k in range(1, n):
            to = peer(third, k)
            send(mid2.at[p, to[third]], got3.at[p, k - 1], rs.at[2], rr.at[6 + p], device(to, core))

    out = []
    for p in range(3):
        wait_bytes(got3.at[p], rr.at[6 + p])
        own = mid2[p, coord[ORDERS[p][2]]]
        out.append(merge(p, [own] + [got3[p, k - 1] for k in range(1, n)]))

    lane = lane_of(QB)
    a, b, c = out
    total = c[:, L_LANE : L_LANE + 1]
    b_back = pltpu.roll(b, 96, 1)
    out_ref[:, 0:LANES] = jnp.where(lane < 96, a, b_back) / total
    out_ref[:, LANES:PREFIX] = jnp.where(lane < 64, b_back, pltpu.roll(c, 64, 1)) / total
    lse = c[:, M_LANE:] * math.log(2.0) + jnp.log(total)
    full = pltpu.roll(c, LANES - F_LANE, 1) * width ** (-0.5)
    out_ref[:, PREFIX : PREFIX + LANES] = full - lse
    out_ref[:, PREFIX + LANES :] = jnp.broadcast_to(lse, (QB, LANES))

    for phase in range(4):
        wait_bytes(x_buf.at[(slice(None),) + phase_box(phase)], xs.at[phase])
        for p in range(3):
            wait_bytes(f_bufs[p].at[phase_box(phase)], fs.at[p * 4 + phase])
    for t in range(pairs):
        wait_bytes(pay.at[t], s0.at[t])
    wait_bytes(got1, rs.at[0])
    wait_bytes(got2, rs.at[1])
    wait_bytes(got3, rs.at[2])


def split(in_ref, pooled_ref, lse_ref, margin_ref):
    pooled_ref[...] = in_ref[:, 0:PREFIX]
    margin_ref[...] = in_ref[:, PREFIX : PREFIX + margin_ref.shape[1]]
    here = lax.broadcasted_iota(jnp.int32, (QB, LANES), 0) == lane_of(QB)
    lse = jnp.sum(jnp.where(here, in_ref[:, PREFIX + LANES :], 0.0), axis=0, keepdims=True)
    lse_ref[...] = lse[:, 0:QB]


def make(mesh, dims):
    def on_device(queries, slab, cand_owner, cand_row):
        width = queries.shape[1]
        r_dev = slab.shape[0]
        k_count = cand_owner.shape[1]
        tiles = (width - PREFIX) // LANES
        n0 = -(-tiles // 3)
        n1 = -(-(tiles - n0) // 2)
        col0 = (PREFIX, PREFIX + n0 * LANES, PREFIX + (n0 + n1) * LANES, width)
        n = dims[0]
        chunk = 2 * n * n * QB
        n_slot = chunk // QB * SLOTS
        vmem = pltpu.VMEM
        dma = pltpu.SemaphoreType.DMA
        spec = pl.BlockSpec(memory_space=pltpu.VMEM)
        merged = pl.pallas_call(
            functools.partial(kernel, dims, col0),
            out_shape=jax.ShapeDtypeStruct((QB, PREFIX + 2 * LANES), F32),
            in_specs=[spec, pl.BlockSpec(memory_space=pl.ANY), spec, spec],
            out_specs=spec,
            scratch_shapes=[
                vmem((r_dev, width), BF16),
                vmem((3, n, n, n, 2, QB, LANES), BF16),
                vmem((n, n, n, 2, QB, col0[1] - col0[0]), BF16),
                vmem((n, n, n, 2, QB, col0[2] - col0[1]), BF16),
                vmem((n, n, n, 2, QB, col0[3] - col0[2]), BF16),
                vmem((n, chunk, n_slot), F32),
                vmem((n * n_slot, r_dev), BF16),
                vmem((n * n_slot, width), BF16),
                vmem((chunk, r_dev), F32),
                vmem((n // 2, 3, 2, n, n, QB, LANES), F32),
                vmem((n // 2, 3, 2, n, n, QB, LANES), F32),
                vmem((3, n, n, n, QB, LANES), F32),
                vmem((3, n - 1, n, n, QB, LANES), F32),
                vmem((3, n, n, QB, LANES), F32),
                vmem((3, n - 1, n, QB, LANES), F32),
                vmem((3, n, QB, LANES), F32),
                vmem((3, n - 1, QB, LANES), F32),
                dma((2,)),
                dma((4,)),
                dma((12,)),
                dma((12,)),
                dma((12,)),
                dma((n // 2,)),
                dma((n // 2,)),
                dma((3,)),
                dma((9,)),
            ],
            compiler_params=pltpu.CompilerParams(
                collective_id=0, has_side_effects=True, vmem_limit_bytes=56 * 2**20
            ),
        )(queries, slab, cand_owner, cand_row)
        pooled, lse, margin = pl.pallas_call(
            split,
            out_shape=(
                jax.ShapeDtypeStruct((QB, PREFIX), F32),
                jax.ShapeDtypeStruct((1, QB), F32),
                jax.ShapeDtypeStruct((QB, k_count), F32),
            ),
            in_specs=[spec],
            out_specs=(spec, spec, spec),
        )(merged)
        return pooled, lse.reshape(QB), margin

    both = ("index", "query")
    return jax.shard_map(
        on_device,
        mesh=mesh,
        in_specs=(P(both, None),) * 4,
        out_specs=(P(both, None), P(both), P(both, None)),
        check_vma=False,
    )


def solution(mesh):
    side = math.isqrt(mesh.shape["index"])
    return make(mesh, (side, side, mesh.shape["query"] // 2))
```

time: 72 us -> 63.3 us (0.88)
  Pallas kernels: 67.3 us -> 62.5 us
  local copies, waits for them, and re-layouts: 2.56 us -> 0 us
  other arithmetic: 1.3 us -> 0 us
    pallas_call x1 -> x2, Pallas kernels: 67.3 us -> 62.5 us  [the longest x1 61.1 us: on_device(): pl.pallas_call(functools.partial(kernel, dims, col0), out_shape=jax.Shape...]
    unnamed x2 -> x0, local copies, waits for them, and re-layouts: 2.56 us -> none
    pallas_call x1 -> x0, other arithmetic: 1.3 us -> none  [on_device(): pl.pallas_call(functools.partial(kernel, dims, col0), out_shape=(jax.Shap...]
where the time goes in v2:
time: 63.3 us; the launch traced here: 63.1 us
  Pallas kernels  62.5 us (99%)
  between operations  0.64 us (1%)
    pallas_call x1, Pallas kernels, on_device(): pl.pallas_call(functools.partial(kernel, dims, col0), out_shape=jax.Shape...  61.1 us
    pallas_call x1, Pallas kernels, on_device(): pl.pallas_call(split, out_shape=(jax.ShapeDtypeStruct((QB, PREFIX), F32),...  1.33 us

profile of v2, /device:TPU:0, one launch (start us, length us, event | category | flops | bytes accessed | tf_op | source)
XLA Modules:
  0.0 63.1 jit_solution(15955062820442264732)
XLA Ops:
  0.6 61.1 %shard_map.67.in_ref = f32[8,512]{1,0:T(8,128)} custom-call(bf16[8,2048]{1,0:T(8,128)(2,1)} %q_ref.1, bf16[4096,2048]{1,0:T(8,128)(2,1)} %slab_ref.1, s32[8,32]{1,0:T(8,128)} %own_ref.1, s32[8,32]{1,0:T(8,128)} %row_ref.1), custom_call_target="tpu_custom_call" | custom-call | tf_op jit(solution)/shard_map/pallas_call | solution.py:415
  61.8 1.3 %shard_map.68 = (f32[8,256]{1,0:T(8,128)}, f32[1,8]{1,0:T(1,128)}, f32[8,32]{1,0:T(8,128)}) custom-call(f32[8,512]{1,0:T(8,128)} %shard_map.67.in_ref), custom_call_target="tpu_custom_call" | custom-call | tf_op jit(solution)/shard_map/pallas_call | solution.py:452

commit v3 on v2

--- a/solution.py
+++ b/solution.py
@@ -43,18 +43,22 @@
     col0,
     q_ref,
     slab_ref,
+    groups_ref,
     own_ref,
     row_ref,
     out_ref,
+    pre_v,
     slab_v,
     x_buf,
     f0,
     f1,
     f2,
     sel_buf,
-    hot,
+    idx_v,
+    idx_s,
     rows_buf,
     logits,
+    tops,
     pay,
     got0,
     mid0,
@@ -98,14 +102,8 @@
 
     sibling = device(coord, 1 - core)
 
-    pre_copy = pltpu.make_async_copy(
-        slab_ref.at[:, pl.ds(0, PREFIX)], slab_v.at[:, pl.ds(0, PREFIX)], lsem.at[0]
-    )
-    rest_copy = pltpu.make_async_copy(
-        slab_ref.at[:, pl.ds(PREFIX, width - PREFIX)],
-        slab_v.at[:, pl.ds(PREFIX, width - PREFIX)],
-        lsem.at[1],
-    )
+    pre_copy = pltpu.make_async_copy(slab_ref.at[:, pl.ds(0, PREFIX)], pre_v, lsem.at[0])
+    rest_copy = pltpu.make_async_copy(groups_ref, slab_v, lsem.at[1])
 
     barrier = pltpu.get_barrier_semaphore()
     pl.semaphore_signal(barrier, inc=1, device_id=sibling, device_id_type=pl.DeviceIdType.MESH)
@@ -229,109 +227,132 @@
         )
         sel_buf[j] = sel
         picked = jnp.dot(
-            sel.T.astype(BF16),
-            jnp.where(lane < 64, high, low).astype(BF16),
+            jnp.where(lane < 64, high, low).T.astype(BF16),
+            sel.astype(BF16),
             preferred_element_type=F32,
         )
-        row_of = (picked[:, 0:1] * 64.0 + picked[:, 64:65]).astype(jnp.int32)
-        rows = pl.ds(pl.multiple_of(j * n_slot, n_slot), n_slot)
-        for u in range(r_dev // 512):
-            r = lax.broadcasted_iota(jnp.int32, (n_slot, 512), 1) + u * 512
-            hot[rows, u * 512 : (u + 1) * 512] = jnp.where(r == row_of, 1.0, 0.0).astype(BF16)
-
-    @pl.loop(0, pairs)
-    def _(t):
-        index(t, t, core)
-
-    x_step(3)
-
-    @pl.loop(0, pairs)
-    def _(t):
-        index(pairs + t, t, 1 - core)
-
+        row_of = (picked[0:1, :] * 64.0 + picked[64:65, :]).astype(jnp.int32)
+        idx_v[pl.ds(j, 1), 0:n_slot] = row_of
+
+    def half_of(j):
+        return lax.rem(j, pairs), jnp.where(j < pairs, core, 1 - core)
+
+    @pl.loop(0, n)
+    def _(j):
+        @pl.when(j == pairs)
+        def _():
+            x_step(3)
+
+        index(j, *half_of(j))
+
+    idx_copy = pltpu.make_async_copy(idx_v, idx_s, lsem.at[2])
+    idx_copy.start()
     pre_copy.wait()
-    rest_copy.wait()
-
-    def pick_rows(i):
-        cols = pl.ds(pl.multiple_of(i * 256, 256), 256)
-        rows_buf[:, cols] = jnp.dot(hot[...], slab_v[:, cols], preferred_element_type=F32).astype(BF16)
-
-    half = width // 512
-
-    @pl.loop(0, half)
-    def _(i):
-        pick_rows(i)
-
-    f_step(2)
-
-    @pl.loop(half, width // 256)
-    def _(i):
-        pick_rows(i)
-
-    f_step(3)
 
     factor = PREFIX ** (-0.5) * math.log2(math.e)
     tile = 512
 
-    def score(j, t, c):
-        q = jnp.concatenate([part_of(x_bufs[0], t, c), part_of(x_bufs[1], t, c)], axis=1).astype(BF16)
+    def prefix_of(j):
+        t, c = half_of(j)
+        return jnp.concatenate([part_of(x_bufs[0], t, c), part_of(x_bufs[1], t, c)], axis=1).astype(BF16)
+
+    @pl.loop(0, n)
+    def _(j):
+        q = prefix_of(j)
         most = jnp.full((chunk, LANES), -jnp.inf, F32)
         for u in range(r_dev // tile):
             s = lax.dot_general(
-                q, slab_v[u * tile : (u + 1) * tile, 0:PREFIX], NT, preferred_element_type=F32
+                q, pre_v[u * tile : (u + 1) * tile, :], NT, preferred_element_type=F32
             )
-            logits[:, u * tile : (u + 1) * tile] = s
+            logits[j, :, u * tile : (u + 1) * tile] = s
             for v in range(tile // LANES):
                 most = jnp.maximum(most, s[:, v * LANES : (v + 1) * LANES])
-        top = jnp.max(most, axis=1, keepdims=True) * factor
+        tops[j] = jnp.broadcast_to(jnp.max(most, axis=1, keepdims=True) * factor, (chunk, LANES))
+
+    idx_copy.wait()
+    rest_copy.wait()
+
+    @pl.loop(0, n * n_slot // QB)
+    def _(g):
+        sub = lax.broadcasted_iota(jnp.int32, (QB, width), 0)
+        rows = jnp.zeros((QB, width), F32)
+        for k in range(QB):
+            at = g * QB + k
+            i = jnp.clip(idx_s[lax.div(at, n_slot), lax.rem(at, n_slot)], 0, r_dev - 1)
+            group = slab_v[i >> 3].astype(F32)
+            rows = jnp.where(sub == k, pltpu.roll(group, (k - (i & 7)) & 7, 0), rows)
+        rows_buf[g] = rows
+
+    f_step(2)
+
+    @pl.loop(0, n)
+    def _(jj):
+        j = lax.rem(jj + pairs, n)
+        top = tops[j][:, 0:1]
         total = jnp.zeros((chunk, LANES), F32)
         acc = jnp.zeros((chunk, PREFIX), F32)
         for u in range(r_dev // tile):
-            w = jnp.exp2(logits[:, u * tile : (u + 1) * tile] * factor - top)
+            w = jnp.exp2(logits[j, :, u * tile : (u + 1) * tile] * factor - top)
             for v in range(tile // LANES):
                 total = total + w[:, v * LANES : (v + 1) * LANES]
             acc = acc + jnp.dot(
-                w.astype(BF16), slab_v[u * tile : (u + 1) * tile, 0:PREFIX], preferred_element_type=F32
+                w.astype(BF16), pre_v[u * tile : (u + 1) * tile, :], preferred_element_type=F32
             )
         total = jnp.sum(total, axis=1, keepdims=True)
-
-        rows = pl.ds(pl.multiple_of(j * n_slot, n_slot), n_slot)
-        scores = lax.dot_general(q, rows_buf[rows, 0:PREFIX], NT, preferred_element_type=F32)
+        lane = lane_of(chunk)
+        p0, p1 = acc[:, :LANES], acc[:, LANES:]
+        b = jnp.where(lane < 32, pltpu.roll(p0, 32, 1), pltpu.roll(p1, 32, 1))
+        c = jnp.where(lane < F_LANE, pltpu.roll(p1, 64, 1), 0.0)
+        c = jnp.where(lane == L_LANE, total, c)
+        for p, v in enumerate((p0, b, c)):
+            pay[j, p] = jnp.where(lane == M_LANE, top, v).reshape(box)
+
+        @pl.when(jj < pairs)
+        def _():
+            send(pay.at[j, pl.ds(0, 2)], got0.at[jj, pl.ds(0, 2)], s0.at[jj], r0.at[jj], sibling)
+
+    f_step(3)
+
+    @pl.loop(0, n)
+    def _(jj):
+        j = lax.rem(jj + pairs, n)
+        t, c = half_of(j)
+        groups = pl.ds(j * (n_slot // QB), n_slot // QB)
+
+        def rows_of(lo, hi):
+            return rows_buf[groups, :, lo:hi].reshape(n_slot, hi - lo).astype(BF16)
+
+        scores = lax.dot_general(prefix_of(j), rows_of(0, PREFIX), NT, preferred_element_type=F32)
         for p in range(3):
             scores = scores + lax.dot_general(
                 part_of(f_bufs[p], t, c).astype(BF16),
-                rows_buf[rows, col0[p] : col0[p + 1]],
+                rows_of(col0[p], col0[p + 1]),
                 NT,
                 preferred_element_type=F32,
             )
         full = jnp.sum(scores * sel_buf[j], axis=1, keepdims=True)
-
         lane = lane_of(chunk)
         full = jnp.where((part_of(x_bufs[2], t, c) == me_f) & (lane < k_count), full, 0.0)
-        p0, p1 = acc[:, :LANES], acc[:, LANES:]
-        b = jnp.where(lane < 32, pltpu.roll(p0, 32, 1), pltpu.roll(p1, 32, 1))
-        c = jnp.where(lane < F_LANE, pltpu.roll(p1, 64, 1), pltpu.roll(full, F_LANE, 1))
-        c = jnp.where(lane == L_LANE, total, c)
-        return [jnp.where(lane == M_LANE, top, v) for v in (p0, b, c)]
-
-    @pl.loop(0, pairs)
-    def _(t):
-        for p, v in enumerate(score(pairs + t, t, 1 - core)):
-            pay[t, p] = v.reshape(box)
-        send(pay.at[t], got0.at[t], s0.at[t], r0.at[t], sibling)
-
-    @pl.loop(0, pairs)
-    def _(t):
-        mine = score(t, t, core)
-        wait_bytes(got0.at[t], r0.at[t])
-        for p in range(3):
-            both = merge(p, [mine[p], got0[t, p].reshape(chunk, LANES)])
-            mid0[p, pl.ds(2 * t, 2)] = both.reshape(box)
+        pay[j, 2] = pay[j, 2] + pltpu.roll(full, F_LANE, 1).reshape(box)
+
+        @pl.when(jj < pairs)
+        def _():
+            send(pay.at[j, 2], got0.at[jj, 2], s0.at[pairs + jj], r0.at[pairs + jj], sibling)
 
     def at_axis(axes, axis, index):
         return tuple(index if a == axis else slice(None) for a in axes)
 
     for p in range(3):
+
+        @pl.loop(0, pairs)
+        def _(t, p=p):
+            if p == 0:
+                wait_bytes(got0.at[t, pl.ds(0, 2)], r0.at[t])
+            elif p == 2:
+                wait_bytes(got0.at[t, 2], r0.at[pairs + t])
+            both = merge(p, [pay[t, p].reshape(chunk, LANES), got0[t, p].reshape(chunk, LANES)])
+            mid0[p, pl.ds(2 * t, 2)] = both.reshape(box)
+
         axis = ORDERS[p][0]
         for k in range(1, n):
             to = peer(axis, k)
@@ -383,7 +404,8 @@
         for p in range(3):
             wait_bytes(f_bufs[p].at[phase_box(phase)], fs.at[p * 4 + phase])
     for t in range(pairs):
-        wait_bytes(pay.at[t], s0.at[t])
+        wait_bytes(got0.at[t, pl.ds(0, 2)], s0.at[t])
+        wait_bytes(got0.at[t, 2], s0.at[pairs + t])
     wait_bytes(got1, rs.at[0])
     wait_bytes(got2, rs.at[1])
     wait_bytes(got3, rs.at[2])
@@ -415,40 +437,43 @@
         merged = pl.pallas_call(
             functools.partial(kernel, dims, col0),
             out_shape=jax.ShapeDtypeStruct((QB, PREFIX + 2 * LANES), F32),
-            in_specs=[spec, pl.BlockSpec(memory_space=pl.ANY), spec, spec],
+            in_specs=[spec, pl.BlockSpec(memory_space=pl.ANY), pl.BlockSpec(memory_space=pl.ANY), spec, spec],
             out_specs=spec,
             scratch_shapes=[
-                vmem((r_dev, width), BF16),
+                vmem((r_dev, PREFIX), BF16),
+                vmem((r_dev // QB, QB, width), BF16),
                 vmem((3, n, n, n, 2, QB, LANES), BF16),
                 vmem((n, n, n, 2, QB, col0[1] - col0[0]), BF16),
                 vmem((n, n, n, 2, QB, col0[2] - col0[1]), BF16),
                 vmem((n, n, n, 2, QB, col0[3] - col0[2]), BF16),
                 vmem((n, chunk, n_slot), F32),
-                vmem((n * n_slot, r_dev), BF16),
-                vmem((n * n_slot, width), BF16),
-                vmem((chunk, r_dev), F32),
-                vmem((n // 2, 3, 2, n, n, QB, LANES), F32),
-                vmem((n // 2, 3, 2, n, n, QB, LANES), F32),
+                vmem((QB, LANES), jnp.int32),
+                pltpu.SMEM((QB, LANES), jnp.int32),
+                vmem((n * n_slot // QB, QB, width), F32),
+                vmem((n, chunk, r_dev), F32),
+                vmem((n, chunk, LANES), F32),
+                vmem((n, 3) + (2, n, n, QB, LANES), F32),
+                vmem((n // 2, 3) + (2, n, n, QB, LANES), F32),
                 vmem((3, n, n, n, QB, LANES), F32),
                 vmem((3, n - 1, n, n, QB, LANES), F32),
                 vmem((3, n, n, QB, LANES), F32),
                 vmem((3, n - 1, n, QB, LANES), F32),
                 vmem((3, n, QB, LANES), F32),
                 vmem((3, n - 1, QB, LANES), F32),
-                dma((2,)),
+                dma((3,)),
                 dma((4,)),
                 dma((12,)),
                 dma((12,)),
                 dma((12,)),
-                dma((n // 2,)),
-                dma((n // 2,)),
+                dma((n,)),
+                dma((n,)),
                 dma((3,)),
                 dma((9,)),
             ],
             compiler_params=pltpu.CompilerParams(
                 collective_id=0, has_side_effects=True, vmem_limit_bytes=56 * 2**20
             ),
-        )(queries, slab, cand_owner, cand_row)
+        )(queries, slab, slab.reshape(r_dev // QB, QB, width), cand_owner, cand_row)
         pooled, lse, margin = pl.pallas_call(
             split,
             out_shape=(

time: 63.3 us -> 56.1 us (0.89)
  Pallas kernels: 62.5 us -> 55.3 us
    pallas_call x1, Pallas kernels: 61.1 us -> 54 us  [on_device(): pl.pallas_call(functools.partial(kernel, dims, col0), out_shape=jax.Shape...]
where the time goes in v3:
time: 56.1 us; the launch traced here: 55.9 us
  Pallas kernels  55.3 us (99%)
  between operations  0.64 us (1%)
    pallas_call x1, Pallas kernels, on_device(): pl.pallas_call(functools.partial(kernel, dims, col0), out_shape=jax.Shape...  54 us
    pallas_call x1, Pallas kernels, on_device(): pl.pallas_call(split, out_shape=(jax.ShapeDtypeStruct((QB, PREFIX), F32),...  1.33 us

profile of v3, /device:TPU:0, one launch (start us, length us, event | category | flops | bytes accessed | tf_op | source)
XLA Modules:
  0.0 55.9 jit_solution(9173051976186057728)
XLA Ops:
  0.6 54.0 %shard_map.67.in_ref = f32[8,512]{1,0:T(8,128)} custom-call(bf16[8,2048]{1,0:T(8,128)(2,1)} %q_ref.1, bf16[4096,2048]{1,0:T(8,128)(2,1)} %slab_ref.1, bf16[512,8,2048]{2,1,0:T(8,128)(2,1)} %bitcast.2, s32[8,32]{1,0:T(8,128)} %own_ref.1, s32[8,32]{1,0:T(8,128)} %row_ref.1), custom_call_target="tpu_custom_call" | custom-call | tf_op jit(solution)/shard_map/pallas_call | solution.py:437
  54.6 1.3 %shard_map.68 = (f32[8,256]{1,0:T(8,128)}, f32[1,8]{1,0:T(1,128)}, f32[8,32]{1,0:T(8,128)}) custom-call(f32[8,512]{1,0:T(8,128)} %shard_map.67.in_ref), custom_call_target="tpu_custom_call" | custom-call | tf_op jit(solution)/shard_map/pallas_call | solution.py:477

commit v4 on v3

--- a/solution.py
+++ b/solution.py
@@ -54,9 +54,11 @@
     f1,
     f2,
     sel_buf,
+    sel_got,
     idx_v,
     idx_s,
     rows_buf,
+    rows_got,
     logits,
     tops,
     pay,
@@ -72,6 +74,8 @@
     xr,
     fs,
     fr,
+    ws,
+    wr,
     s0,
     r0,
     rs,
@@ -130,7 +134,7 @@
     )
     x_buf[(2,) + here] = numbers.astype(BF16)
     for p in range(3):
-        f_bufs[p][here] = q_ref[:, col0[p] : col0[p + 1]]
+        f_bufs[p][coord] = q_ref[:, col0[p] : col0[p + 1]]
     pl.semaphore_wait(barrier, 1 + 3 * (n - 1))
 
     def send(src, dst, ssem, rsem, target):
@@ -148,58 +152,52 @@
 
     def phase_box(phase):
         if phase == 3:
-            return (slice(None),) * 3 + (0,)
-        return (slice(0, n - 1),) + (slice(None),) * phase + (0,) * (2 - phase) + (0,)
-
-    def gather_start(bufs, ssem_of, rsem, phase, p):
+            return (slice(None),) * 3
+        return (slice(0, n - 1),) + (slice(None),) * phase + (0,) * (2 - phase)
+
+    def gather_start(buf, tail, ssem, rsem, phase, p):
         if phase == 3:
-            block = bufs[p].at[:, :, :, core]
+            block = buf.at[(slice(None),) * 3 + tail]
             targets = [sibling]
         else:
             done = ORDERS[p][:phase]
             where = tuple(slice(None) if a in done else coord[a] for a in range(3))
-            block = bufs[p].at[where + (core,)]
+            block = buf.at[where + tail]
             axis = ORDERS[p][phase]
             targets = [device(peer(axis, k), core) for k in range(1, n)]
         for target in targets:
-            send(block, block, ssem_of(p, phase), rsem.at[p * 4 + phase], target)
-
-    def x_ssem(p, phase):
-        return xs.at[phase]
-
-    def f_ssem(p, phase):
-        return fs.at[p * 4 + phase]
-
-    def x_start(phase):
-        for p in range(3):
-            gather_start(x_bufs, x_ssem, xr, phase, p)
-
-    def f_start(phase):
-        for p in range(3):
-            gather_start(f_bufs, f_ssem, fr, phase, p)
+            send(block, block, ssem, rsem, target)
+
+    def x_start(phase, p):
+        gather_start(x_bufs[p], (core,), xs.at[phase], xr.at[p * 4 + phase], phase, p)
+
+    def f_start(phase, p):
+        gather_start(f_bufs[p], (), fs.at[p * 3 + phase], fr.at[p * 3 + phase], phase, p)
 
     def x_step(phase):
         for p in range(3):
-            wait_bytes(x_bufs[p].at[phase_box(phase)], xr.at[p * 4 + phase])
+            wait_bytes(x_bufs[p].at[phase_box(phase) + (0,)], xr.at[p * 4 + phase])
             if phase < 3:
-                gather_start(x_bufs, x_ssem, xr, phase + 1, p)
+                x_start(phase + 1, p)
 
     def f_step(phase):
         for p in range(3):
-            wait_bytes(f_bufs[p].at[phase_box(phase)], fr.at[p * 4 + phase])
-            if phase < 3:
-                gather_start(f_bufs, f_ssem, fr, phase + 1, p)
-
-    x_start(0)
-    f_start(0)
+            wait_bytes(f_bufs[p].at[phase_box(phase)], fr.at[p * 3 + phase])
+            if phase < 2:
+                f_start(phase + 1, p)
+
+    for p in range(3):
+        x_start(0, p)
+    for p in range(3):
+        f_start(0, p)
     x_step(0)
     x_step(1)
     f_step(0)
     x_step(2)
     f_step(1)
 
-    def part_of(buf, t, c):
-        v = buf[pl.ds(2 * t, 2), :, :, c]
+    def part_of(buf, t, *c):
+        v = buf[(pl.ds(2 * t, 2), slice(None), slice(None)) + c]
         return v.astype(F32).reshape(chunk, v.shape[-1])
 
     def index(j, t, c):
@@ -247,6 +245,7 @@
 
     idx_copy = pltpu.make_async_copy(idx_v, idx_s, lsem.at[2])
     idx_copy.start()
+    send(sel_buf.at[pl.ds(pairs, pairs)], sel_got, ws.at[0], wr.at[0], sibling)
     pre_copy.wait()
 
     factor = PREFIX ** (-0.5) * math.log2(math.e)
@@ -272,18 +271,25 @@
     idx_copy.wait()
     rest_copy.wait()
 
-    @pl.loop(0, n * n_slot // QB)
-    def _(g):
-        sub = lax.broadcasted_iota(jnp.int32, (QB, width), 0)
-        rows = jnp.zeros((QB, width), F32)
-        for k in range(QB):
-            at = g * QB + k
-            i = jnp.clip(idx_s[lax.div(at, n_slot), lax.rem(at, n_slot)], 0, r_dev - 1)
-            group = slab_v[i >> 3].astype(F32)
-            rows = jnp.where(sub == k, pltpu.roll(group, (k - (i & 7)) & 7, 0), rows)
-        rows_buf[g] = rows
-
-    f_step(2)
+    half = pairs * n_slot // QB
+
+    @pl.loop(0, 2)
+    def _(h):
+        @pl.loop(0, half)
+        def _(gg):
+            g = (1 - h) * half + gg
+            sub = lax.broadcasted_iota(jnp.int32, (QB, width), 0)
+            rows = jnp.zeros((QB, width), F32)
+            for k in range(QB):
+                at = g * QB + k
+                i = jnp.clip(idx_s[lax.div(at, n_slot), lax.rem(at, n_slot)], 0, r_dev - 1)
+                group = slab_v[i >> 3].astype(F32)
+                rows = jnp.where(sub == k, pltpu.roll(group, (k - (i & 7)) & 7, 0), rows)
+            rows_buf[g] = rows.astype(BF16)
+
+        @pl.when(h == 0)
+        def _():
+            send(rows_buf.at[pl.ds(half, half)], rows_got, ws.at[1], wr.at[1], sibling)
 
     @pl.loop(0, n)
     def _(jj):
@@ -309,35 +315,37 @@
 
         @pl.when(jj < pairs)
         def _():
-            send(pay.at[j, pl.ds(0, 2)], got0.at[jj, pl.ds(0, 2)], s0.at[jj], r0.at[jj], sibling)
-
-    f_step(3)
-
-    @pl.loop(0, n)
-    def _(jj):
-        j = lax.rem(jj + pairs, n)
-        t, c = half_of(j)
-        groups = pl.ds(j * (n_slot // QB), n_slot // QB)
-
+            send(pay.at[j], got0.at[jj], s0.at[jj], r0.at[jj], sibling)
+
+    f_step(2)
+    wait_bytes(sel_got, wr.at[0])
+    wait_bytes(rows_got, wr.at[1])
+
+    sibling_f = me_f + (1 - 2 * core).astype(F32)
+    step = n_slot // QB
+
+    @pl.loop(0, pairs)
+    def _(t):
         def rows_of(lo, hi):
-            return rows_buf[groups, :, lo:hi].reshape(n_slot, hi - lo).astype(BF16)
-
-        scores = lax.dot_general(prefix_of(j), rows_of(0, PREFIX), NT, preferred_element_type=F32)
+            groups = pl.ds(t * step, step)
+            mine = rows_buf[groups, :, lo:hi].astype(F32).reshape(n_slot, hi - lo)
+            other = rows_got[groups, :, lo:hi].astype(F32).reshape(n_slot, hi - lo)
+            return jnp.concatenate([mine, other], axis=0).astype(BF16)
+
+        scores = lax.dot_general(prefix_of(t), rows_of(0, PREFIX), NT, preferred_element_type=F32)
         for p in range(3):
             scores = scores + lax.dot_general(
-                part_of(f_bufs[p], t, c).astype(BF16),
+                part_of(f_bufs[p], t).astype(BF16),
                 rows_of(col0[p], col0[p + 1]),
                 NT,
                 preferred_element_type=F32,
             )
-        full = jnp.sum(scores * sel_buf[j], axis=1, keepdims=True)
         lane = lane_of(chunk)
-        full = jnp.where((part_of(x_bufs[2], t, c) == me_f) & (lane < k_count), full, 0.0)
-        pay[j, 2] = pay[j, 2] + pltpu.roll(full, F_LANE, 1).reshape(box)
-
-        @pl.when(jj < pairs)
-        def _():
-            send(pay.at[j, 2], got0.at[jj, 2], s0.at[pairs + jj], r0.at[pairs + jj], sibling)
+        numbers = jnp.where(lane < k_count, part_of(x_bufs[2], t, core), -1.0)
+        full = jnp.sum(scores[:, :n_slot] * sel_buf[t], axis=1, keepdims=True)
+        full2 = jnp.sum(scores[:, n_slot:] * sel_got[t], axis=1, keepdims=True)
+        full = jnp.where(numbers == me_f, full, jnp.where(numbers == sibling_f, full2, 0.0))
+        pay[t, 2] = pay[t, 2] + pltpu.roll(full, F_LANE, 1).reshape(box)
 
     def at_axis(axes, axis, index):
         return tuple(index if a == axis else slice(None) for a in axes)
@@ -347,9 +355,7 @@
         @pl.loop(0, pairs)
         def _(t, p=p):
             if p == 0:
-                wait_bytes(got0.at[t, pl.ds(0, 2)], r0.at[t])
-            elif p == 2:
-                wait_bytes(got0.at[t, 2], r0.at[pairs + t])
+                wait_bytes(got0.at[t], r0.at[t])
             both = merge(p, [pay[t, p].reshape(chunk, LANES), got0[t, p].reshape(chunk, LANES)])
             mid0[p, pl.ds(2 * t, 2)] = both.reshape(box)
 
@@ -400,12 +406,14 @@
     out_ref[:, PREFIX + LANES :] = jnp.broadcast_to(lse, (QB, LANES))
 
     for phase in range(4):
-        wait_bytes(x_buf.at[(slice(None),) + phase_box(phase)], xs.at[phase])
+        wait_bytes(x_buf.at[(slice(None),) + phase_box(phase) + (0,)], xs.at[phase])
+    for phase in range(3):
         for p in range(3):
-            wait_bytes(f_bufs[p].at[phase_box(phase)], fs.at[p * 4 + phase])
+            wait_bytes(f_bufs[p].at[phase_box(phase)], fs.at[p * 3 + phase])
+    wait_bytes(sel_got, ws.at[0])
+    wait_bytes(rows_got, ws.at[1])
     for t in range(pairs):
-        wait_bytes(got0.at[t, pl.ds(0, 2)], s0.at[t])
-        wait_bytes(got0.at[t, 2], s0.at[pairs + t])
+        wait_bytes(got0.at[t], s0.at[t])
     wait_bytes(got1, rs.at[0])
     wait_bytes(got2, rs.at[1])
     wait_bytes(got3, rs.at[2])
@@ -443,13 +451,15 @@
                 vmem((r_dev, PREFIX), BF16),
                 vmem((r_dev // QB, QB, width), BF16),
                 vmem((3, n, n, n, 2, QB, LANES), BF16),
-                vmem((n, n, n, 2, QB, col0[1] - col0[0]), BF16),
-                vmem((n, n, n, 2, QB, col0[2] - col0[1]), BF16),
-                vmem((n, n, n, 2, QB, col0[3] - col0[2]), BF16),
+                vmem((n, n, n, QB, col0[1] - col0[0]), BF16),
+                vmem((n, n, n, QB, col0[2] - col0[1]), BF16),
+                vmem((n, n, n, QB, col0[3] - col0[2]), BF16),
                 vmem((n, chunk, n_slot), F32),
+                vmem((n // 2, chunk, n_slot), F32),
                 vmem((QB, LANES), jnp.int32),
                 pltpu.SMEM((QB, LANES), jnp.int32),
-                vmem((n * n_slot // QB, QB, width), F32),
+                vmem((n * n_slot // QB, QB, width), BF16),
+                vmem((n * n_slot // QB // 2, QB, width), BF16),
                 vmem((n, chunk, r_dev), F32),
                 vmem((n, chunk, LANES), F32),
                 vmem((n, 3) + (2, n, n, QB, LANES), F32),
@@ -463,10 +473,12 @@
                 dma((3,)),
                 dma((4,)),
                 dma((12,)),
-                dma((12,)),
-                dma((12,)),
-                dma((n,)),
-                dma((n,)),
+                dma((9,)),
+                dma((9,)),
+                dma((2,)),
+                dma((2,)),
+                dma((n // 2,)),
+                dma((n // 2,)),
                 dma((3,)),
                 dma((9,)),
             ],

time: 56.1 us -> 55.2 us (0.984)
  Pallas kernels: 55.3 us -> 54.3 us
    pallas_call x1, Pallas kernels: 54 us -> 53 us  [on_device(): pl.pallas_call(functools.partial(kernel, dims, col0), out_shape=jax.Shape...]
where the time goes in v4:
time: 55.2 us; the launch traced here: 55 us
  Pallas kernels  54.3 us (98%)
  between operations  0.64 us (1%)
    pallas_call x1, Pallas kernels, on_device(): pl.pallas_call(functools.partial(kernel, dims, col0), out_shape=jax.Shape...  53 us
    pallas_call x1, Pallas kernels, on_device(): pl.pallas_call(split, out_shape=(jax.ShapeDtypeStruct((QB, PREFIX), F32),...  1.33 us

profile of v4, /device:TPU:0, one launch (start us, length us, event | category | flops | bytes accessed | tf_op | source)
XLA Modules:
  0.0 55.0 jit_solution(6309194137390507540)
XLA Ops:
  0.6 53.0 %shard_map.67.in_ref = f32[8,512]{1,0:T(8,128)} custom-call(bf16[8,2048]{1,0:T(8,128)(2,1)} %q_ref.1, bf16[4096,2048]{1,0:T(8,128)(2,1)} %slab_ref.1, bf16[512,8,2048]{2,1,0:T(8,128)(2,1)} %bitcast.2, s32[8,32]{1,0:T(8,128)} %own_ref.1, s32[8,32]{1,0:T(8,128)} %row_ref.1), custom_call_target="tpu_custom_call" | custom-call | tf_op jit(solution)/shard_map/pallas_call | solution.py:445
  53.7 1.3 %shard_map.68 = (f32[8,256]{1,0:T(8,128)}, f32[1,8]{1,0:T(1,128)}, f32[8,32]{1,0:T(8,128)}) custom-call(f32[8,512]{1,0:T(8,128)} %shard_map.67.in_ref), custom_call_target="tpu_custom_call" | custom-call | tf_op jit(solution)/shard_map/pallas_call | solution.py:489

commit v5 on v4

--- a/solution.py
+++ b/solution.py
@@ -67,8 +67,6 @@
     got1,
     mid1,
     got2,
-    mid2,
-    got3,
     lsem,
     xs,
     xr,
@@ -99,9 +97,13 @@
     def device(at, c):
         return (at[0] * n + at[1], at[2] * 2 + c)
 
-    def peer(axis, k):
+    moved = [[coord[a]] + [lax.rem(coord[a] + k, n) for k in range(1, n)] for a in range(3)]
+
+    def peer(axis, k, axis2=None, k2=0):
         at = list(coord)
-        at[axis] = lax.rem(coord[axis] + k, n)
+        at[axis] = moved[axis][k]
+        if axis2 is not None:
+            at[axis2] = moved[axis2][k2]
         return tuple(at)
 
     sibling = device(coord, 1 - core)
@@ -111,11 +113,12 @@
 
     barrier = pltpu.get_barrier_semaphore()
     pl.semaphore_signal(barrier, inc=1, device_id=sibling, device_id_type=pl.DeviceIdType.MESH)
-    for axis in range(3):
-        for k in range(1, n):
-            pl.semaphore_signal(
-                barrier, inc=1, device_id=device(peer(axis, k), core), device_id_type=pl.DeviceIdType.MESH
-            )
+    near = [peer(a, k) for a in range(3) for k in range(1, n)]
+    near += [peer(a, k, b, k2) for a in range(3) for b in range(a) for k in range(1, n) for k2 in range(1, n)]
+    for at in near:
+        pl.semaphore_signal(
+            barrier, inc=1, device_id=device(at, core), device_id_type=pl.DeviceIdType.MESH
+        )
     pre_copy.start()
     rest_copy.start()
 
@@ -135,7 +138,7 @@
     x_buf[(2,) + here] = numbers.astype(BF16)
     for p in range(3):
         f_bufs[p][coord] = q_ref[:, col0[p] : col0[p + 1]]
-    pl.semaphore_wait(barrier, 1 + 3 * (n - 1))
+    pl.semaphore_wait(barrier, 1 + len(near))
 
     def send(src, dst, ssem, rsem, target):
         pltpu.make_async_remote_copy(
@@ -174,9 +177,22 @@
     def f_start(phase, p):
         gather_start(f_bufs[p], (), fs.at[p * 3 + phase], fr.at[p * 3 + phase], phase, p)
 
+    def x_plane(p):
+        block = x_bufs[p].at[here]
+        first, second = ORDERS[p][:2]
+        for k2 in range(n):
+            for k in range(0 if k2 else 1, n):
+                at = min(k2, 1)
+                send(block, block, xs.at[at], xr.at[p * 4 + at], device(peer(first, k, second, k2), core))
+
+    def x_wait(phase, p):
+        wait_bytes(x_bufs[p].at[phase_box(phase) + (0,)], xr.at[p * 4 + phase])
+
     def x_step(phase):
         for p in range(3):
-            wait_bytes(x_bufs[p].at[phase_box(phase) + (0,)], xr.at[p * 4 + phase])
+            if phase == 1:
+                x_wait(0, p)
+            x_wait(phase, p)
             if phase < 3:
                 x_start(phase + 1, p)
 
@@ -187,10 +203,9 @@
                 f_start(phase + 1, p)
 
     for p in range(3):
-        x_start(0, p)
+        x_plane(p)
     for p in range(3):
         f_start(0, p)
-    x_step(0)
     x_step(1)
     f_step(0)
     x_step(2)
@@ -367,32 +382,22 @@
     flat1 = (n * n * QB, LANES)
     for p in range(3):
         wait_bytes(got1.at[p], rr.at[p])
-        first, second, third = ORDERS[p]
+        first = ORDERS[p][0]
         own = mid0[(p,) + at_axis(range(3), first, coord[first])].reshape(flat1)
         blocks = [own] + [got1[p, k - 1].reshape(flat1) for k in range(1, n)]
         mid1[p] = merge(p, blocks).reshape(n, n, QB, LANES)
         left = [a for a in range(3) if a != first]
-        for k in range(1, n):
-            to = peer(second, k)
-            send(mid1.at[(p,) + at_axis(left, second, to[second])], got2.at[p, k - 1], rs.at[1], rr.at[3 + p], device(to, core))
-
-    flat2 = (n * QB, LANES)
+        for k in range(n * n - 1):
+            k2, k3 = (k + 1) // n, (k + 1) % n
+            to = peer(left[0], k2, left[1], k3)
+            send(mid1.at[p, to[left[0]], to[left[1]]], got2.at[p, k], rs.at[1], rr.at[3 + p], device(to, core))
+
+    out = []
     for p in range(3):
         wait_bytes(got2.at[p], rr.at[3 + p])
-        first, second, third = ORDERS[p]
-        left = [a for a in range(3) if a != first]
-        own = mid1[(p,) + at_axis(left, second, coord[second])].reshape(flat2)
-        blocks = [own] + [got2[p, k - 1].reshape(flat2) for k in range(1, n)]
-        mid2[p] = merge(p, blocks).reshape(n, QB, LANES)
-        for k in range(1, n):
-            to = peer(third, k)
-            send(mid2.at[p, to[third]], got3.at[p, k - 1], rs.at[2], rr.at[6 + p], device(to, core))
-
-    out = []
-    for p in range(3):
-        wait_bytes(got3.at[p], rr.at[6 + p])
-        own = mid2[p, coord[ORDERS[p][2]]]
-        out.append(merge(p, [own] + [got3[p, k - 1] for k in range(1, n)]))
+        left = [coord[a] for a in range(3) if a != ORDERS[p][0]]
+        own = mid1[p, left[0], left[1]]
+        out.append(merge(p, [own] + [got2[p, k] for k in range(n * n - 1)]))
 
     lane = lane_of(QB)
     a, b, c = out
@@ -416,7 +421,6 @@
         wait_bytes(got0.at[t], s0.at[t])
     wait_bytes(got1, rs.at[0])
     wait_bytes(got2, rs.at[1])
-    wait_bytes(got3, rs.at[2])
 
 
 def split(in_ref, pooled_ref, lse_ref, margin_ref):
@@ -467,9 +471,7 @@
                 vmem((3, n, n, n, QB, LANES), F32),
                 vmem((3, n - 1, n, n, QB, LANES), F32),
                 vmem((3, n, n, QB, LANES), F32),
-                vmem((3, n - 1, n, QB, LANES), F32),
-                vmem((3, n, QB, LANES), F32),
-                vmem((3, n - 1, QB, LANES), F32),
+                vmem((3, n * n - 1, QB, LANES), F32),
                 dma((3,)),
                 dma((4,)),
                 dma((12,)),
@@ -479,8 +481,8 @@
                 dma((2,)),
                 dma((n // 2,)),
                 dma((n // 2,)),
-                dma((3,)),
-                dma((9,)),
+                dma((2,)),
+                dma((6,)),
             ],
             compiler_params=pltpu.CompilerParams(
                 collective_id=0, has_side_effects=True, vmem_limit_bytes=56 * 2**20

time: 55.2 us -> 50.2 us (0.909)
  Pallas kernels: 54.3 us -> 49.3 us
    pallas_call x1, Pallas kernels: 53 us -> 48 us  [on_device(): pl.pallas_call(functools.partial(kernel, dims, col0), out_shape=jax.Shape...]
where the time goes in v5:
time: 50.2 us; the launch traced here: 50 us
  Pallas kernels  49.3 us (98%)
  between operations  0.64 us (1%)
    pallas_call x1, Pallas kernels, on_device(): pl.pallas_call(functools.partial(kernel, dims, col0), out_shape=jax.Shape...  48 us
    pallas_call x1, Pallas kernels, on_device(): pl.pallas_call(split, out_shape=(jax.ShapeDtypeStruct((QB, PREFIX), F32),...  1.33 us

profile of v5, /device:TPU:0, one launch (start us, length us, event | category | flops | bytes accessed | tf_op | source)
XLA Modules:
  0.0 50.0 jit_solution(1307368129143709613)
XLA Ops:
  0.6 48.0 %shard_map.67.in_ref = f32[8,512]{1,0:T(8,128)} custom-call(bf16[8,2048]{1,0:T(8,128)(2,1)} %q_ref.1, bf16[4096,2048]{1,0:T(8,128)(2,1)} %slab_ref.1, bf16[512,8,2048]{2,1,0:T(8,128)(2,1)} %bitcast.2, s32[8,32]{1,0:T(8,128)} %own_ref.1, s32[8,32]{1,0:T(8,128)} %row_ref.1), custom_call_target="tpu_custom_call" | custom-call | tf_op jit(solution)/shard_map/pallas_call | solution.py:449
  48.6 1.3 %shard_map.68 = (f32[8,256]{1,0:T(8,128)}, f32[1,8]{1,0:T(1,128)}, f32[8,32]{1,0:T(8,128)}) custom-call(f32[8,512]{1,0:T(8,128)} %shard_map.67.in_ref), custom_call_target="tpu_custom_call" | custom-call | tf_op jit(solution)/shard_map/pallas_call | solution.py:491

commit v6 on v5

--- a/solution.py
+++ b/solution.py
@@ -107,6 +107,7 @@
         return tuple(at)
 
     sibling = device(coord, 1 - core)
+    far_first = sorted(range(1, n), key=lambda k: -min(k, n - k))
 
     pre_copy = pltpu.make_async_copy(slab_ref.at[:, pl.ds(0, PREFIX)], pre_v, lsem.at[0])
     rest_copy = pltpu.make_async_copy(groups_ref, slab_v, lsem.at[1])
@@ -167,7 +168,7 @@
             where = tuple(slice(None) if a in done else coord[a] for a in range(3))
             block = buf.at[where + tail]
             axis = ORDERS[p][phase]
-            targets = [device(peer(axis, k), core) for k in range(1, n)]
+            targets = [device(peer(axis, k), core) for k in far_first]
         for target in targets:
             send(block, block, ssem, rsem, target)
 
@@ -250,17 +251,7 @@
     def half_of(j):
         return lax.rem(j, pairs), jnp.where(j < pairs, core, 1 - core)
 
-    @pl.loop(0, n)
-    def _(j):
-        @pl.when(j == pairs)
-        def _():
-            x_step(3)
-
-        index(j, *half_of(j))
-
     idx_copy = pltpu.make_async_copy(idx_v, idx_s, lsem.at[2])
-    idx_copy.start()
-    send(sel_buf.at[pl.ds(pairs, pairs)], sel_got, ws.at[0], wr.at[0], sibling)
     pre_copy.wait()
 
     factor = PREFIX ** (-0.5) * math.log2(math.e)
@@ -270,18 +261,35 @@
         t, c = half_of(j)
         return jnp.concatenate([part_of(x_bufs[0], t, c), part_of(x_bufs[1], t, c)], axis=1).astype(BF16)
 
-    @pl.loop(0, n)
-    def _(j):
-        q = prefix_of(j)
-        most = jnp.full((chunk, LANES), -jnp.inf, F32)
-        for u in range(r_dev // tile):
-            s = lax.dot_general(
-                q, pre_v[u * tile : (u + 1) * tile, :], NT, preferred_element_type=F32
-            )
-            logits[j, :, u * tile : (u + 1) * tile] = s
-            for v in range(tile // LANES):
-                most = jnp.maximum(most, s[:, v * LANES : (v + 1) * LANES])
-        tops[j] = jnp.broadcast_to(jnp.max(most, axis=1, keepdims=True) * factor, (chunk, LANES))
+    @pl.loop(0, 2)
+    def _(h):
+        @pl.when(h == 1)
+        def _():
+            x_step(3)
+
+        @pl.loop(0, pairs)
+        def _(t):
+            j = h * pairs + t
+            index(j, *half_of(j))
+
+        @pl.when(h == 1)
+        def _():
+            idx_copy.start()
+            send(sel_buf.at[pl.ds(pairs, pairs)], sel_got, ws.at[0], wr.at[0], sibling)
+
+        @pl.loop(0, pairs)
+        def _(t):
+            j = h * pairs + t
+            q = prefix_of(j)
+            most = jnp.full((chunk, LANES), -jnp.inf, F32)
+            for u in range(r_dev // tile):
+                s = lax.dot_general(
+                    q, pre_v[u * tile : (u + 1) * tile, :], NT, preferred_element_type=F32
+                )
+                logits[j, :, u * tile : (u + 1) * tile] = s
+                for v in range(tile // LANES):
+                    most = jnp.maximum(most, s[:, v * LANES : (v + 1) * LANES])
+            tops[j] = jnp.broadcast_to(jnp.max(most, axis=1, keepdims=True) * factor, (chunk, LANES))
 
     idx_copy.wait()
     rest_copy.wait()
@@ -375,7 +383,7 @@
             mid0[p, pl.ds(2 * t, 2)] = both.reshape(box)
 
         axis = ORDERS[p][0]
-        for k in range(1, n):
+        for k in far_first:
             to = peer(axis, k)
             send(mid0.at[(p,) + at_axis(range(3), axis, to[axis])], got1.at[p, k - 1], rs.at[0], rr.at[p], device(to, core))
 

time: 50.2 us -> 50.2 us (level)
  no operation moved by 1% of the time
where the time goes in v6:
time: 50.2 us; the launch traced here: 50 us
  Pallas kernels  49.3 us (98%)
  between operations  0.64 us (1%)
    pallas_call x1, Pallas kernels, on_device(): pl.pallas_call(functools.partial(kernel, dims, col0), out_shape=jax.Shape...  48 us
    pallas_call x1, Pallas kernels, on_device(): pl.pallas_call(split, out_shape=(jax.ShapeDtypeStruct((QB, PREFIX), F32),...  1.33 us

profile of v6, /device:TPU:0, one launch (start us, length us, event | category | flops | bytes accessed | tf_op | source)
XLA Modules:
  0.0 50.0 jit_solution(8255297415854529568)
XLA Ops:
  0.6 48.0 %shard_map.67.in_ref = f32[8,512]{1,0:T(8,128)} custom-call(bf16[8,2048]{1,0:T(8,128)(2,1)} %q_ref.1, bf16[4096,2048]{1,0:T(8,128)(2,1)} %slab_ref.1, bf16[512,8,2048]{2,1,0:T(8,128)(2,1)} %bitcast.2, s32[8,32]{1,0:T(8,128)} %own_ref.1, s32[8,32]{1,0:T(8,128)} %row_ref.1), custom_call_target="tpu_custom_call" | custom-call | tf_op jit(solution)/shard_map/pallas_call | solution.py:457
  48.6 1.3 %shard_map.68 = (f32[8,256]{1,0:T(8,128)}, f32[1,8]{1,0:T(1,128)}, f32[8,32]{1,0:T(8,128)}) custom-call(f32[8,512]{1,0:T(8,128)} %shard_map.67.in_ref), custom_call_target="tpu_custom_call" | custom-call | tf_op jit(solution)/shard_map/pallas_call | solution.py:499

commit v7 on v6

--- a/solution.py
+++ b/solution.py
@@ -256,6 +256,7 @@
 
     factor = PREFIX ** (-0.5) * math.log2(math.e)
     tile = 512
+    side = pairs * chunk
 
     def prefix_of(j):
         t, c = half_of(j)
@@ -277,19 +278,16 @@
             idx_copy.start()
             send(sel_buf.at[pl.ds(pairs, pairs)], sel_got, ws.at[0], wr.at[0], sibling)
 
-        @pl.loop(0, pairs)
-        def _(t):
-            j = h * pairs + t
-            q = prefix_of(j)
-            most = jnp.full((chunk, LANES), -jnp.inf, F32)
-            for u in range(r_dev // tile):
-                s = lax.dot_general(
-                    q, pre_v[u * tile : (u + 1) * tile, :], NT, preferred_element_type=F32
-                )
-                logits[j, :, u * tile : (u + 1) * tile] = s
-                for v in range(tile // LANES):
-                    most = jnp.maximum(most, s[:, v * LANES : (v + 1) * LANES])
-            tops[j] = jnp.broadcast_to(jnp.max(most, axis=1, keepdims=True) * factor, (chunk, LANES))
+        q = jnp.concatenate([prefix_of(h * pairs + t) for t in range(pairs)], axis=0)
+        most = jnp.full((side, LANES), -jnp.inf, F32)
+        for u in range(r_dev // tile):
+            s = lax.dot_general(
+                q, pre_v[u * tile : (u + 1) * tile, :], NT, preferred_element_type=F32
+            )
+            logits[h, :, u * tile : (u + 1) * tile] = s
+            for v in range(tile // LANES):
+                most = jnp.maximum(most, s[:, v * LANES : (v + 1) * LANES])
+        tops[h] = jnp.broadcast_to(jnp.max(most, axis=1, keepdims=True) * factor, (side, LANES))
 
     idx_copy.wait()
     rest_copy.wait()
@@ -298,7 +296,7 @@
 
     @pl.loop(0, 2)
     def _(h):
-        @pl.loop(0, half)
+        @pl.loop(0, half, unroll=4)
         def _(gg):
             g = (1 - h) * half + gg
             sub = lax.broadcasted_iota(jnp.int32, (QB, width), 0)
@@ -314,31 +312,32 @@
         def _():
             send(rows_buf.at[pl.ds(half, half)], rows_got, ws.at[1], wr.at[1], sibling)
 
-    @pl.loop(0, n)
-    def _(jj):
-        j = lax.rem(jj + pairs, n)
-        top = tops[j][:, 0:1]
-        total = jnp.zeros((chunk, LANES), F32)
-        acc = jnp.zeros((chunk, PREFIX), F32)
+    @pl.loop(0, 2)
+    def _(hh):
+        h = 1 - hh
+        top = tops[h][:, 0:1]
+        total = jnp.zeros((side, LANES), F32)
+        acc = jnp.zeros((side, PREFIX), F32)
         for u in range(r_dev // tile):
-            w = jnp.exp2(logits[j, :, u * tile : (u + 1) * tile] * factor - top)
+            w = jnp.exp2(logits[h, :, u * tile : (u + 1) * tile] * factor - top)
             for v in range(tile // LANES):
                 total = total + w[:, v * LANES : (v + 1) * LANES]
             acc = acc + jnp.dot(
                 w.astype(BF16), pre_v[u * tile : (u + 1) * tile, :], preferred_element_type=F32
             )
         total = jnp.sum(total, axis=1, keepdims=True)
-        lane = lane_of(chunk)
+        lane = lane_of(side)
         p0, p1 = acc[:, :LANES], acc[:, LANES:]
         b = jnp.where(lane < 32, pltpu.roll(p0, 32, 1), pltpu.roll(p1, 32, 1))
         c = jnp.where(lane < F_LANE, pltpu.roll(p1, 64, 1), 0.0)
         c = jnp.where(lane == L_LANE, total, c)
         for p, v in enumerate((p0, b, c)):
-            pay[j, p] = jnp.where(lane == M_LANE, top, v).reshape(box)
-
-        @pl.when(jj < pairs)
+            pay[pl.ds(h * pairs, pairs), p] = jnp.where(lane == M_LANE, top, v).reshape((pairs,) + box)
+
+        @pl.when(hh == 0)
         def _():
-            send(pay.at[j], got0.at[jj], s0.at[jj], r0.at[jj], sibling)
+            for t in range(pairs):
+                send(pay.at[pairs + t], got0.at[t], s0.at[t], r0.at[t], sibling)
 
     f_step(2)
     wait_bytes(sel_got, wr.at[0])
@@ -472,8 +471,8 @@
                 pltpu.SMEM((QB, LANES), jnp.int32),
                 vmem((n * n_slot // QB, QB, width), BF16),
                 vmem((n * n_slot // QB // 2, QB, width), BF16),
-                vmem((n, chunk, r_dev), F32),
-                vmem((n, chunk, LANES), F32),
+                vmem((2, n // 2 * chunk, r_dev), F32),
+                vmem((2, n // 2 * chunk, LANES), F32),
                 vmem((n, 3) + (2, n, n, QB, LANES), F32),
                 vmem((n // 2, 3) + (2, n, n, QB, LANES), F32),
                 vmem((3, n, n, n, QB, LANES), F32),

time: 50.2 us -> 48.1 us (0.958)
  Pallas kernels: 49.3 us -> 47.3 us
    pallas_call x1, Pallas kernels: 48 us -> 46 us  [on_device(): pl.pallas_call(functools.partial(kernel, dims, col0), out_shape=jax.Shape...]
where the time goes in v7:
time: 48.1 us; the launch traced here: 47.9 us
  Pallas kernels  47.3 us (98%)
  between operations  0.64 us (1%)
    pallas_call x1, Pallas kernels, on_device(): pl.pallas_call(functools.partial(kernel, dims, col0), out_shape=jax.Shape...  46 us
    pallas_call x1, Pallas kernels, on_device(): pl.pallas_call(split, out_shape=(jax.ShapeDtypeStruct((QB, PREFIX), F32),...  1.33 us

profile of v7, /device:TPU:0, one launch (start us, length us, event | category | flops | bytes accessed | tf_op | source)
XLA Modules:
  0.0 47.9 jit_solution(1158954862726137564)
XLA Ops:
  0.6 46.0 %shard_map.67.in_ref = f32[8,512]{1,0:T(8,128)} custom-call(bf16[8,2048]{1,0:T(8,128)(2,1)} %q_ref.1, bf16[4096,2048]{1,0:T(8,128)(2,1)} %slab_ref.1, bf16[512,8,2048]{2,1,0:T(8,128)(2,1)} %bitcast.2, s32[8,32]{1,0:T(8,128)} %own_ref.1, s32[8,32]{1,0:T(8,128)} %row_ref.1), custom_call_target="tpu_custom_call" | custom-call | tf_op jit(solution)/shard_map/pallas_call | solution.py:456
  46.6 1.3 %shard_map.68 = (f32[8,256]{1,0:T(8,128)}, f32[1,8]{1,0:T(1,128)}, f32[8,32]{1,0:T(8,128)}) custom-call(f32[8,512]{1,0:T(8,128)} %shard_map.67.in_ref), custom_call_target="tpu_custom_call" | custom-call | tf_op jit(solution)/shard_map/pallas_call | solution.py:498

commit v8 on v7

--- a/solution.py
+++ b/solution.py
@@ -346,7 +346,7 @@
     sibling_f = me_f + (1 - 2 * core).astype(F32)
     step = n_slot // QB
 
-    @pl.loop(0, pairs)
+    @pl.loop(0, pairs, unroll=pairs)
     def _(t):
         def rows_of(lo, hi):
             groups = pl.ds(t * step, step)
@@ -374,7 +374,7 @@
 
     for p in range(3):
 
-        @pl.loop(0, pairs)
+        @pl.loop(0, pairs, unroll=pairs)
         def _(t, p=p):
             if p == 0:
                 wait_bytes(got0.at[t], r0.at[t])

time: 48.1 us -> 47.5 us (0.988)
  Pallas kernels: 47.3 us -> 46.6 us
    pallas_call x1, Pallas kernels: 46 us -> 45.3 us  [on_device(): pl.pallas_call(functools.partial(kernel, dims, col0), out_shape=jax.Shape...]
where the time goes in v8:
time: 47.5 us; the launch traced here: 47.3 us
  Pallas kernels  46.6 us (98%)
  between operations  0.64 us (1%)
    pallas_call x1, Pallas kernels, on_device(): pl.pallas_call(functools.partial(kernel, dims, col0), out_shape=jax.Shape...  45.3 us
    pallas_call x1, Pallas kernels, on_device(): pl.pallas_call(split, out_shape=(jax.ShapeDtypeStruct((QB, PREFIX), F32),...  1.33 us

profile of v8, /device:TPU:0, one launch (start us, length us, event | category | flops | bytes accessed | tf_op | source)
XLA Modules:
  0.0 47.3 jit_solution(673484209629283362)
XLA Ops:
  0.6 45.3 %shard_map.67.in_ref = f32[8,512]{1,0:T(8,128)} custom-call(bf16[8,2048]{1,0:T(8,128)(2,1)} %q_ref.1, bf16[4096,2048]{1,0:T(8,128)(2,1)} %slab_ref.1, bf16[512,8,2048]{2,1,0:T(8,128)(2,1)} %bitcast.2, s32[8,32]{1,0:T(8,128)} %own_ref.1, s32[8,32]{1,0:T(8,128)} %row_ref.1), custom_call_target="tpu_custom_call" | custom-call | tf_op jit(solution)/shard_map/pallas_call | solution.py:456
  46.0 1.3 %shard_map.68 = (f32[8,256]{1,0:T(8,128)}, f32[1,8]{1,0:T(1,128)}, f32[8,32]{1,0:T(8,128)}) custom-call(f32[8,512]{1,0:T(8,128)} %shard_map.67.in_ref), custom_call_target="tpu_custom_call" | custom-call | tf_op jit(solution)/shard_map/pallas_call | solution.py:498
